TPU v7x, 32 devices: a whole 2x2x4 slice. The times are simulated.
32 devices in a mesh: groups: 2 (over y), row: 8 (over z, x), col: 2 (over core).
Axes of the slice: x: 2, y: 2, z: 4, core: 2. Of those that a mesh axis runs over, the one named last changes fastest.
Arguments:
- hidden_states: bfloat16 [32, 6144], P(('groups', 'row'), 'col'), parts along dimension 0, may hold values from -6 to 6
- scale_attn: float32 [6144], P('col'), may hold values from 0.5 to 1.5
- w_qkv: bfloat16 [6144, 18432], P('col', 'row'), may hold values from -0.078125 to 0.078125
- w_out: bfloat16 [6144, 6144], P('col', 'row'), may hold values from -0.078125 to 0.078125
- scale_mlp: float32 [6144], P('col'), may hold values from 0.5 to 1.5
- w_gate: bfloat16 [6144, 24576], P('col', 'row'), may hold values from -0.078125 to 0.078125
- w_up: bfloat16 [6144, 24576], P('col', 'row'), may hold values from -0.078125 to 0.078125
- w_down: bfloat16 [24576, 6144], P('row', 'col'), may hold values from -0.0390625 to 0.0390625
Outputs:
- updated: bfloat16 [32, 6144], P(('groups', 'row'), 'col'), parts along dimension 0
There are 2 independent parts, one for each index of `groups`. A program takes and returns all parts, laid end to end along the dimension named above; an argument that names none is the same for every part. Nothing has to cross between parts.
All inputs are finite; a program needn't handle non-finite values.
Results may differ from a plain program's by a relative error of at most 0.015.
Values may be sent and summed in bfloat16 or wider, within the bound.
No kernel may reach another device: no remote copies, remote signals or barrier semaphores. Data moves between devices by JAX's collectives and lax.ppermute only.
A program may use at most 192 MiB of HBM per device.

v0:
```python
import math

import jax
import jax.numpy as jnp
from jax import lax
from jax.sharding import PartitionSpec as P

HEADS = 48
HS = 128
D = 6144


EPSILON = 1e-06


def project(section, weight):
    return jnp.dot(section, weight, preferred_element_type=jnp.float32)


def to_rows(partial_sum, tok_rows):
    groups = lax.axis_size("col")
    row_count = lax.axis_size("row")
    half_rows = tok_rows // groups
    columns = partial_sum.shape[1]
    ordered = (
        partial_sum.reshape(row_count, groups, half_rows, columns)
        .transpose(1, 0, 2, 3)
        .reshape(-1, columns)
    )
    summed = lax.psum_scatter(ordered.astype(jnp.bfloat16), "col", scatter_dimension=0, tiled=True)
    return lax.all_to_all(
        lax.all_to_all(summed, "row", split_axis=0, concat_axis=1, tiled=True),
        "col",
        split_axis=1,
        concat_axis=0,
        tiled=True,
    )


def per_device(hidden_states, scale_attn, w_qkv, w_out, scale_mlp, w_gate, w_up, w_down):
    tok_rows = hidden_states.shape[0]
    groups = lax.axis_size("col")
    stream = hidden_states.astype(jnp.float32)
    totals = lax.psum(jnp.sum(stream * stream, axis=-1), "col")
    normed = (stream * lax.rsqrt(totals / D + EPSILON)[:, None] * scale_attn).astype(jnp.bfloat16)
    qkv_partial = project(lax.all_gather(normed, "row", axis=0, tiled=True), weight=w_qkv)
    qkv = to_rows(qkv_partial, tok_rows)
    local_heads = HEADS // groups
    head_cols = local_heads * HS
    queries = qkv[:, :head_cols].reshape(tok_rows, local_heads, HS)
    key_rows = qkv[:, head_cols : 2 * head_cols]
    value_rows = qkv[:, 2 * head_cols :]
    factor = 1.0 / math.sqrt(HS)
    running = jnp.full((local_heads, tok_rows), -1e30, jnp.float32)
    key_piece = lax.all_gather(key_rows, "row", axis=0, tiled=True).reshape(-1, local_heads, HS)
    value_piece = lax.all_gather(value_rows, "row", axis=0, tiled=True).reshape(-1, local_heads, HS)
    scores = (
        jnp.einsum("qhd,khd->hqk", queries, key_piece, preferred_element_type=jnp.float32) * factor
    )
    new_max = jnp.maximum(running, jnp.max(scores, axis=-1))
    weights = jnp.exp(scores - new_max[..., None])
    weight_sum = jnp.sum(weights, axis=-1)
    numerator = jnp.einsum(
        "hqk,khd->hqd",
        weights.astype(jnp.bfloat16),
        value_piece,
        preferred_element_type=jnp.float32,
    )
    running, weight_sum, numerator = (new_max, weight_sum, numerator)
    attended = (
        (numerator / weight_sum[..., None])
        .transpose(1, 0, 2)
        .reshape(tok_rows, head_cols)
        .astype(jnp.bfloat16)
    )
    out_partial = project(lax.all_gather(attended, "row", axis=0, tiled=True), weight=w_out)
    attn_out = to_rows(out_partial, tok_rows)
    resid = stream + attn_out.astype(jnp.float32)
    totals2 = lax.psum(jnp.sum(resid * resid, axis=-1), "col")
    normed2 = (resid * lax.rsqrt(totals2 / D + EPSILON)[:, None] * scale_mlp).astype(jnp.bfloat16)
    section = lax.all_gather(normed2, "row", axis=0, tiled=True)
    gate_up = jnp.concatenate(
        [
            jnp.dot(section, w_gate, preferred_element_type=jnp.float32),
            jnp.dot(section, w_up, preferred_element_type=jnp.float32),
        ],
        axis=1,
    )
    unit_count = w_gate.shape[1]
    share_sum = lax.psum_scatter(
        gate_up.astype(jnp.bfloat16), "col", scatter_dimension=0, tiled=True
    ).astype(jnp.float32)
    part_hidden = (jax.nn.silu(share_sum[:, :unit_count]) * share_sum[:, unit_count:]).astype(
        jnp.bfloat16
    )
    hidden = lax.all_gather(part_hidden, "col", axis=0, tiled=True)
    lowered = lax.psum_scatter(
        jnp.dot(hidden, w_down, preferred_element_type=jnp.float32),
        "row",
        scatter_dimension=0,
        tiled=True,
    )
    return (resid + lowered).astype(jnp.bfloat16)


def solution(mesh):
    return jax.shard_map(
        per_device,
        mesh=mesh,
        in_specs=(
            P(("groups", "row"), "col"),
            P("col"),
            P("col", "row"),
            P("col", "row"),
            P("col"),
            P("col", "row"),
            P("col", "row"),
            P("row", "col"),
        ),
        out_specs=P(("groups", "row"), "col"),
        check_vma=False,
    )
```

profile of v0, /device:TPU:0, one launch (start us, length us, event | category | flops | bytes accessed | tf_op | source)
XLA Modules:
  0.0 346.3 jit_solution(3833287077309690215)
XLA Ops:
  7.5 2.6 psum.14
  10.9 32.2 %all-gather = bf16[8,2,3072]{2,1,0:T(2,128)(2,1)S(1)} all-gather(bf16[1,2,3072]{2,1,0:T(2,128)(2,1)S(1)} %fusion.14), channel_id=1, replica_groups=mesh['groups'=2,'row'=8,'col'=2] {'row'}, dimensions={0}, use_global_device_ids=true | all-gather | bytes 110592 | tf_op jit(solution)/shard_map/all_gather | solution.py:46
  43.1 7.0 %convolution_convert_fusion.2 = bf16[16,2304]{1,0:T(8,128)(2,1)S(1)} fusion(bf16[16,3072]{1,0:T(8,128)(2,1)S(1)} %reshape.60, bf16[3072,2304]{1,0:T(8,128)(2,1)} %param.10), kind=kOutput, calls=%fused_computation.2 | convolution fusion | flops 226529280 | bytes 14327808 | tf_op jit(solution)/shard_map/dot_general | solution.py:17
  50.8 8.5 %reduce-scatter.4.cloned.1.call-done = bf16[8,2304]{1,0:T(8,128)(2,1)} async-done(((bf16[16,2304]{1,0:T(8,128)(2,1)}), bf16[8,2304]{1,0:T(8,128)(2,1)}) %reduce-scatter.4.cloned.1.call-update) | async-done | bytes 36880 | tf_op jit(solution)/shard_map/reduce_scatter | solution.py:30
  59.8 1.4 reduce
  61.3 12.3 %all_to_all.55 = bf16[8,2,1152]{2,1,0:T(2,128)(2,1)S(1)} all-to-all(bf16[8,2,1152]{2,1,0:T(2,128)(2,1)S(1)} %reshape.73), channel_id=1, replica_groups=mesh['groups'=2,'row'=8,'col'=2] {'row'}, dimensions={0} | all-to-all | bytes 73728 | tf_op jit(solution)/shard_map/all_to_all | solution.py:32
  74.5 3.8 %all_to_all.56 = bf16[2,2,4608]{2,1,0:T(2,128)(2,1)S(1)} all-to-all(bf16[2,2,4608]{2,1,0:T(2,128)(2,1)S(1)} %reshape.75), channel_id=1, replica_groups=mesh['groups'=2,'row'=8,'col'=2] {'col'}, dimensions={0} | all-to-all | bytes 73728 | tf_op jit(solution)/shard_map/all_to_all | solution.py:31
  78.3 30.5 %all-gather.1 = bf16[8,2,3072]{2,1,0:T(2,128)(2,1)S(1)} all-gather(bf16[1,2,3072]{2,1,0:T(2,128)(2,1)S(1)} %get-tuple-element.5), channel_id=1, replica_groups=mesh['groups'=2,'row'=8,'col'=2] {'row'}, dimensions={0}, use_global_device_ids=true | all-gather | bytes 110592 | tf_op jit(solution)/shard_map/all_gather | solution.py:55
  109.2 30.5 %all-gather.2 = bf16[8,2,3072]{2,1,0:T(2,128)(2,1)S(1)} all-gather(bf16[1,2,3072]{2,1,0:T(2,128)(2,1)S(1)} %get-tuple-element.6), channel_id=1, replica_groups=mesh['groups'=2,'row'=8,'col'=2] {'row'}, dimensions={0}, use_global_device_ids=true | all-gather | bytes 110592 | tf_op jit(solution)/shard_map/all_gather | solution.py:56
  140.2 30.5 %all-gather.3 = bf16[8,2,3072]{2,1,0:T(2,128)(2,1)S(1)} all-gather(bf16[1,2,3072]{2,1,0:T(2,128)(2,1)S(1)} %fusion.2), channel_id=1, replica_groups=mesh['groups'=2,'row'=8,'col'=2] {'row'}, dimensions={0}, use_global_device_ids=true | all-gather | bytes 110592 | tf_op jit(solution)/shard_map/all_gather | solution.py:76
  170.8 3.1 convolution_convert_fusion.3
  174.6 4.9 %reduce-scatter.6.cloned.1.call-done = bf16[8,768]{1,0:T(8,128)(2,1)} async-done(((bf16[16,768]{1,0:T(8,128)(2,1)}), bf16[8,768]{1,0:T(8,128)(2,1)}) %reduce-scatter.6.cloned.1.call-update) | async-done | bytes 12304 | tf_op jit(solution)/shard_map/reduce_scatter | solution.py:30
  179.5 1.4 reduce.2
  180.8 12.1 %all_to_all.57 = bf16[8,2,384]{2,1,0:T(2,128)(2,1)S(1)} all-to-all(bf16[8,2,384]{2,1,0:T(2,128)(2,1)S(1)} %reshape.77), channel_id=1, replica_groups=mesh['groups'=2,'row'=8,'col'=2] {'row'}, dimensions={0} | all-to-all | bytes 24576 | tf_op jit(solution)/shard_map/all_to_all | solution.py:32
  193.7 3.7 %all_to_all.58 = bf16[2,2,1536]{2,1,0:T(2,128)(2,1)S(1)} all-to-all(bf16[2,2,1536]{2,1,0:T(2,128)(2,1)S(1)} %reshape.79), channel_id=1, replica_groups=mesh['groups'=2,'row'=8,'col'=2] {'col'}, dimensions={0} | all-to-all | bytes 24576 | tf_op jit(solution)/shard_map/all_to_all | solution.py:31
  197.6 2.5 psum.15
  200.1 30.6 %all-gather.4 = bf16[8,2,3072]{2,1,0:T(2,128)(2,1)S(1)} all-gather(bf16[1,2,3072]{2,1,0:T(2,128)(2,1)S(1)} %fusion.15), channel_id=1, replica_groups=mesh['groups'=2,'row'=8,'col'=2] {'row'}, dimensions={0}, use_global_device_ids=true | all-gather | bytes 110592 | tf_op jit(solution)/shard_map/all_gather | solution.py:81
  230.7 8.9 %convolution_convert_fusion = bf16[16,3072]{1,0:T(8,128)(2,1)S(1)} fusion(bf16[16,3072]{1,0:T(8,128)(2,1)S(1)} %reshape.68, bf16[3072,3072]{1,0:T(8,128)(2,1)} %param.14), kind=kOutput, calls=%fused_computation | convolution fusion | flops 302039040 | bytes 19070976 | tf_op jit(solution)/shard_map/dot_general | solution.py:85
  239.7 8.9 %convolution_convert_fusion.1 = bf16[16,3072]{1,0:T(8,128)(2,1)S(1)} fusion(bf16[16,3072]{1,0:T(8,128)(2,1)S(1)} %reshape.68, bf16[3072,3072]{1,0:T(8,128)(2,1)} %param.13), kind=kOutput, calls=%fused_computation.1 | convolution fusion | flops 302039040 | bytes 19070976 | tf_op jit(solution)/shard_map/dot_general | solution.py:84
  249.3 4.9 %reduce-scatter.8.cloned.1.call-done = bf16[8,6144]{1,0:T(8,128)(2,1)} async-done(((bf16[16,6144]{1,0:T(8,128)(2,1)}), bf16[8,6144]{1,0:T(8,128)(2,1)}) %reduce-scatter.8.cloned.1.call-update) | async-done | bytes 98320 | tf_op jit(solution)/shard_map/reduce_scatter | solution.py:90
  255.2 2.1 all_gather.23
  257.3 9.6 %fusion.17 = f32[16,3072]{1,0:T(8,128)} fusion(bf16[16,3072]{1,0:T(8,128)(2,1)S(1)} %all_gather.23, bf16[3072,3072]{1,0:T(8,128)(2,1)} %param.15), kind=kOutput, calls=%fused_computation.40 | convolution fusion | flops 301989888 | bytes 19169280 | tf_op jit(solution)/shard_map/dot_general | solution.py:98
  268.2 70.1 %all-reduce.3.cloned.1.call-done = f32[16,3072]{1,0:T(8,128)} async-done(((f32[16,3072]{1,0:T(8,128)}), f32[16,3072]{1,0:T(8,128)}) %all-reduce.3.cloned.1.call-update) | async-done | bytes 196624
  338.3 1.5 fusion.9
  (50 shorter events, 8.9 us)
Async XLA Ops:
  6.5 190.9 %copy-start = (bf16[2,3072]{1,0:T(2,128)(2,1)S(1)}, bf16[2,3072]{1,0:T(2,128)(2,1)}, u32[]{:S(2)}) copy-start(bf16[2,3072]{1,0:T(2,128)(2,1)} %param.8) | copy-start | bytes 36868
  6.5 193.5 %copy-start.1 = (f32[3072]{0:T(1024)S(1)}, f32[3072]{0:T(1024)}, u32[]{:S(2)}) copy-start(f32[3072]{0:T(1024)} %param.12) | copy-start | bytes 36868
  6.5 52.8 %reduce-scatter.4.cloned.1.call-start = ((), (), s32[]{:S(2)}) async-start(), calls=%async_computation.7 | async-start | bytes 110592 | tf_op jit(solution)/shard_map/reduce_scatter | solution.py:30
  50.8 128.7 %reduce-scatter.6.cloned.1.call-start = ((), (), s32[]{:S(2)}) async-start(), calls=%async_computation.8 | async-start | bytes 36864 | tf_op jit(solution)/shard_map/reduce_scatter | solution.py:30
  174.5 79.7 %reduce-scatter.8.cloned.1.call-start = ((), (), s32[]{:S(2)}) async-start(), calls=%async_computation.9 | async-start | bytes 294912 | tf_op jit(solution)/shard_map/reduce_scatter | solution.py:90
  248.6 18.3 %copy-start.2 = (u32[32]{0:T(128)S(1)}, u32[32]{0:T(128)}, u32[]{:S(2)}) copy-start(u32[32]{0:T(128)} %constant.20) | copy-start | bytes 388
  249.3 89.0 %all-reduce.3.cloned.1.call-start = ((), (), s32[]{:S(2)}) async-start(), calls=%async_computation.10 | async-start | bytes 393216
Sparse Core Ops, SparseCore 0:
  50.9 8.3 reduce-scatter.3
  174.7 4.7 reduce-scatter.5
  249.4 4.8 reduce-scatter.7
  267.0 71.1 all-reduce.2
where the time goes:
time: 347 us; the launch traced here: 346 us
  blocking collectives  193 us (56%)
  waiting for transfers between devices  88.5 us (26%)
  matrix products  37.9 us (11%)
  between operations  13.9 us (4%)
  other arithmetic  9.66 us (3%)
    unnamed x5, waiting for transfers between devices  70.2 us
    all_gather x1, blocking collectives, per_device(): lax.all_gather(normed, 'row', axis=0, tiled=True)  32.2 us
    all_gather x1, blocking collectives, per_device(): section = lax.all_gather(normed2, 'row', axis=0, tiled=True)  30.6 us
    all_gather x1, blocking collectives, per_device(): lax.all_gather(key_rows, 'row', axis=0, tiled=True)  30.5 us
    all_gather x1, blocking collectives, per_device(): lax.all_gather(value_rows, 'row', axis=0, tiled=True)  30.5 us
    all_gather x1, blocking collectives, per_device(): lax.all_gather(attended, 'row', axis=0, tiled=True)  30.5 us
    all_to_all x2, blocking collectives, to_rows(): lax.all_to_all(summed, 'row', split_axis=0, concat_axis=1, tiled=True)  24.3 us
    reduce_scatter x2, waiting for transfers between devices, to_rows(): lax.psum_scatter(ordered.astype(jnp.bfloat16), 'col', scatter_dimension=0...  13.4 us
  transfers between devices with their start and end apart: 4, of which 4 were waited for; matrix products, arithmetic and copies ran while one was open for 0% of the time, Pallas kernels for 0%

commit v1 on v0

--- a/solution.py
+++ b/solution.py
@@ -103,9 +103,105 @@
     return (resid + lowered).astype(jnp.bfloat16)
 
 
+def gather_rows(block):
+    row_count = lax.axis_size("row")
+    copies = jnp.broadcast_to(block[None], (row_count,) + block.shape)
+    return lax.all_to_all(copies, "row", split_axis=0, concat_axis=0, tiled=True)
+
+
+def other_core(block):
+    return lax.ppermute(block, "col", [(0, 1), (1, 0)])
+
+
+SQUARE = 4
+
+
+def spread(block):
+    row_count = lax.axis_size("row")
+    mine = lax.axis_index("row")
+    core = lax.axis_index("col")
+    at = lax.rem(mine, SQUARE)
+    home = mine // SQUARE == core
+    got = []
+    for step in range(SQUARE):
+        pairs = []
+        for chip in range(row_count):
+            square, place = chip // SQUARE, chip % SQUARE
+            if step > 0:
+                pairs.append((2 * chip + square, 2 * (SQUARE * square + (place ^ step)) + square))
+            away = 1 - square
+            pairs.append((2 * chip + away, 2 * (SQUARE * away + (place ^ step)) + square))
+        got.append(lax.ppermute(block, ("row", "col"), pairs))
+    got[0] = jnp.where(home, block, got[0])
+    stacked = jnp.stack(got)
+    order = jnp.arange(SQUARE) ^ at
+    return jnp.take(stacked, order, axis=0)
+
+
+def side_by_side(blocks):
+    count, tokens, columns = blocks.shape
+    return blocks.transpose(1, 0, 2).reshape(tokens, count * columns)
+
+
+def few_rows(hidden_states, scale_attn, w_qkv, w_out, scale_mlp, w_gate, w_up, w_down):
+    tok_rows, half = hidden_states.shape
+    row_count = lax.axis_size("row")
+    mine = lax.axis_index("row")
+    tokens = tok_rows * row_count
+    stream = gather_rows(hidden_states).reshape(tokens, half).astype(jnp.float32)
+    squares = jnp.sum(stream * stream, axis=-1, keepdims=True)
+    total = squares + other_core(squares)
+    inverse = lax.rsqrt(total / D + EPSILON)
+    part = project((stream * scale_attn).astype(jnp.bfloat16), w_qkv)
+    qkv = ((part + other_core(part.astype(jnp.bfloat16)).astype(jnp.float32)) * inverse).astype(jnp.bfloat16)
+
+    unit = qkv.shape[1] // 3
+    first, middle, last = qkv[:, :unit], qkv[:, unit : 2 * unit], qkv[:, 2 * unit :]
+    odd = lax.rem(mine, 2) == 1
+    kept = jnp.where(odd, last, first)
+    sent = jnp.where(odd, first, last)
+    from_x = lax.ppermute(middle, "row", [(i, i ^ 1) for i in range(row_count)])
+    from_z = lax.ppermute(sent, "row", [(i, i ^ 2) for i in range(row_count)])
+    at = lax.rem(mine, SQUARE)
+    queries = jnp.where(at == 0, kept, jnp.where(at == 1, from_x, from_z))
+    keys = jnp.where((at == 1) | (at == 2), kept, from_x)
+    values = jnp.where(at == 3, kept, jnp.where(at == 2, from_x, from_z))
+
+    heads = unit // HS
+    queries, keys, values = (v.reshape(tokens, heads, HS) for v in (queries, keys, values))
+    scores = jnp.einsum("qhd,khd->hqk", queries, keys, preferred_element_type=jnp.float32) * (1.0 / math.sqrt(HS))
+    weights = jnp.exp(scores - jnp.max(scores, axis=-1, keepdims=True))
+    mass = jnp.sum(weights, axis=-1, keepdims=True)
+    mixed = jnp.einsum("hqk,khd->hqd", weights.astype(jnp.bfloat16), values, preferred_element_type=jnp.float32) / mass
+    attended = mixed.transpose(1, 0, 2).reshape(tokens, unit).astype(jnp.bfloat16)
+
+    part = project(side_by_side(spread(attended)), w_out)
+    attn_out = (part + other_core(part.astype(jnp.bfloat16)).astype(jnp.float32)).astype(jnp.bfloat16)
+    resid = stream + side_by_side(spread(attn_out)).astype(jnp.float32)
+
+    squares = jnp.sum(resid * resid, axis=-1, keepdims=True)
+    total = squares + other_core(squares)
+    inverse = lax.rsqrt(total / D + EPSILON)
+    section = (resid * scale_mlp).astype(jnp.bfloat16)
+    gate, upward = project(section, w_gate), project(section, w_up)
+    swapped = other_core(jnp.stack([gate, upward]).astype(jnp.bfloat16)).astype(jnp.float32)
+    gate = (gate + swapped[0]) * inverse
+    upward = (upward + swapped[1]) * inverse
+    hidden = (jax.nn.silu(gate) * upward).astype(jnp.bfloat16)
+    lowered = project(hidden, w_down).reshape(row_count, tok_rows, half)
+    lowered = jnp.sum(lax.all_to_all(lowered, "row", split_axis=0, concat_axis=0, tiled=True), axis=0)
+    own = lax.dynamic_slice_in_dim(resid, mine * tok_rows, tok_rows, axis=0)
+    return (own + lowered).astype(jnp.bfloat16)
+
+
+def body(*arrays):
+    fits = lax.axis_size("col") == 2 and lax.axis_size("row") == 2 * SQUARE and HEADS % (2 * SQUARE) == 0
+    return (few_rows if fits else per_device)(*arrays)
+
+
 def solution(mesh):
     return jax.shard_map(
-        per_device,
+        body,
         mesh=mesh,
         in_specs=(
             P(("groups", "row"), "col"),

time: 347 us -> 93.4 us (0.27)
  blocking collectives: 193 us -> 0 us
  waiting for transfers between devices: 88.5 us -> 28.3 us
  starting transfers between devices: 0.13 us -> 29.5 us
  between operations: 13.9 us -> 0.29 us
  matrix products: 37.9 us -> 29.3 us
  other arithmetic: 9.66 us -> 1.62 us
    all_gather x6 -> x0, blocking collectives: 156 us -> none  [the longest x1 32.2 us: per_device(): lax.all_gather(normed, 'row', axis=0, tiled=True)]
    unnamed x5 -> x0, waiting for transfers between devices: 70.2 us -> none
    all_to_all x4 -> x0, blocking collectives: 31.8 us -> none  [the longest x2 24.3 us: to_rows(): lax.all_to_all(summed, 'row', split_axis=0, concat_axis=1, tiled=True)]
    dot_general x5 -> x2, matrix products: 27.9 us -> 0.33 us  [the longest x1 0.2 us: few_rows(): jnp.einsum('hqk,khd->hqd', weights.astype(jnp.bfloat16), values, preferre...]
    dot_general x2 -> x5, matrix products: 10 us -> 29 us  [project(): return jnp.dot(section, weight, preferred_element_type=jnp.float32)]
    ppermute x0 -> x15, starting transfers between devices: none -> 18.8 us  [the longest x5 9.02 us: other_core(): return lax.ppermute(block, 'col', [(0, 1), (1, 0)])]
    reduce_scatter x3 -> x0, waiting for transfers between devices: 18.3 us -> none  [the longest x2 13.4 us: to_rows(): lax.psum_scatter(ordered.astype(jnp.bfloat16), 'col', scatter_dimension=0...]
    all_to_all x0 -> x2, waiting for transfers between devices: none -> 15.6 us  [the longest x1 8.48 us: few_rows(): lax.all_to_all(lowered, 'row', split_axis=0, concat_axis=0, tiled=True)]
  transfers between devices with their start and end apart: 4 -> 17, of which waited for: 4 -> 13; matrix products, arithmetic and copies ran while one was open for 0% -> 25% of each run, Pallas kernels for 0% -> 0%
where the time goes in v1:
time: 93.4 us; the launch traced here: 92.9 us
  starting transfers between devices  29.5 us (32%)
  matrix products  29.3 us (31%)
  waiting for transfers between devices  28.3 us (30%)
  local copies, waits for them, and re-layouts  3.85 us (4%)
  other arithmetic  1.62 us (2%)
    dot_general x5, matrix products, project(): return jnp.dot(section, weight, preferred_element_type=jnp.float32)  29 us
    ppermute x5, starting transfers between devices, other_core(): return lax.ppermute(block, 'col', [(0, 1), (1, 0)])  9.02 us
    all_to_all x1, waiting for transfers between devices, few_rows(): lax.all_to_all(lowered, 'row', split_axis=0, concat_axis=0, tiled=True)  8.48 us
    ppermute x8, starting transfers between devices, spread(): got.append(lax.ppermute(block, ('row', 'col'), pairs))  8.42 us
    all_to_all x1, starting transfers between devices, gather_rows(): lax.all_to_all(copies, 'row', split_axis=0, concat_axis=0, tiled=True)  7.25 us
    all_to_all x1, waiting for transfers between devices, gather_rows(): lax.all_to_all(copies, 'row', split_axis=0, concat_axis=0, tiled=True)  7.12 us
    ppermute x8, waiting for transfers between devices, spread(): got.append(lax.ppermute(block, ('row', 'col'), pairs))  6.89 us
    all_to_all x1, starting transfers between devices, few_rows(): lax.all_to_all(lowered, 'row', split_axis=0, concat_axis=0, tiled=True)  3.51 us
  transfers between devices with their start and end apart: 17, of which 13 were waited for; matrix products, arithmetic and copies ran while one was open for 25% of the time, Pallas kernels for 0%

profile of v1, /device:TPU:0, one launch (start us, length us, event | category | flops | bytes accessed | tf_op | source)
XLA Modules:
  0.0 92.9 jit_solution(15179790250605265611)
XLA Ops:
  0.0 1.4 %broadcast_in_dim.15 = bf16[8,2,3072]{2,1,0:T(2,128)(2,1)} broadcast(bf16[2,3072]{1,0:T(2,128)(2,1)} %param.10), dimensions={1,2} | broadcast | bytes 110592 | tf_op jit(solution)/shard_map/broadcast_in_dim | solution.py:108
  1.4 7.3 %all-to-all-start = ((bf16[8,2,3072]{2,1,0:T(2,128)(2,1)}), bf16[8,2,3072]{2,1,0:T(2,128)(2,1)S(1)}, u32[]{:S(2)}, u32[]{:S(2)}) async-start(bf16[8,2,3072]{2,1,0:T(2,128)(2,1)} %broadcast_in_dim.15), calls=%async_computation | async-start | bytes 196608 | tf_op jit(solution)/shard_map/all_to_all | solution.py:109
  8.7 7.1 %all-to-all-done = bf16[8,2,3072]{2,1,0:T(2,128)(2,1)S(1)} async-done(((bf16[8,2,3072]{2,1,0:T(2,128)(2,1)}), bf16[8,2,3072]{2,1,0:T(2,128)(2,1)S(1)}, u32[]{:S(2)}, u32[]{:S(2)}) %all-to-all-start) | async-done | bytes 98336 | tf_op jit(solution)/shard_map/all_to_all | solution.py:109
  16.1 7.0 %fusion.28 = (bf16[16,2304]{1,0:T(8,128)(2,1)S(1)}, f32[16,2304]{1,0:T(8,128)S(1)}) fusion(bf16[3072,2304]{1,0:T(8,128)(2,1)} %param.12, f32[16,3072]{1,0:T(8,128)S(1)} %reshape.45, f32[3072]{0:T(1024)} %param.11), kind=kOutput, calls=%fused_computation.62 | convolution fusion | flops 226627584 | bytes 14585856 | tf_op jit(solution)/shard_map/dot_general | solution.py:17
  23.6 0.9 collective-permute-done
  24.7 1.2 %collective-permute-start.2 = (bf16[16,768]{1,0:T(8,128)(2,1)S(1)}, bf16[16,768]{1,0:T(8,128)(2,1)S(1)}, u32[]{:S(2)}, u32[]{:S(2)}) collective-permute-start(bf16[16,768]{1,0:T(8,128)(2,1)S(1)} %get-tuple-element.11), channel_id=1, source_target_pairs={{0,2},{2,0},{4,6},{6,4},{8,10},{10,8},{12,14},{14,12},{1,3},{3,1},... | collective-permute-start | bytes 73736 | tf_op jit(solution)/shard_map/ppermute | solution.py:163
  25.9 2.6 %collective-permute-done.3 = bf16[16,768]{1,0:T(8,128)(2,1)S(1)} collective-permute-done((bf16[16,768]{1,0:T(8,128)(2,1)S(1)}, bf16[16,768]{1,0:T(8,128)(2,1)S(1)}, u32[]{:S(2)}, u32[]{:S(2)}) %collective-permute-start.3) | collective-permute-done | bytes 24608 | tf_op jit(solution)/shard_map/ppermute | solution.py:164
  29.7 2.0 %collective-permute-start.6 = (bf16[16,768]{1,0:T(8,128)(2,1)S(1)}, bf16[16,768]{1,0:T(8,128)(2,1)S(1)}, u32[]{:S(2)}, u32[]{:S(2)}) collective-permute-start(bf16[16,768]{1,0:T(8,128)(2,1)S(1)} %bitcast.99), channel_id=1, source_target_pairs={{0,4},{1,12},{2,6},{3,14},{4,0},{5,8},{6,2},{7,10},{9,13},{8,5},{1... | collective-permute-start | bytes 73736 | tf_op jit(solution)/shard_map/ppermute | solution.py:134
  32.0 1.2 %collective-permute-start.7 = (bf16[16,768]{1,0:T(8,128)(2,1)S(1)}, bf16[16,768]{1,0:T(8,128)(2,1)S(1)}, u32[]{:S(2)}, u32[]{:S(2)}) collective-permute-start(bf16[16,768]{1,0:T(8,128)(2,1)S(1)} %bitcast.101), channel_id=1, source_target_pairs={{0,6},{1,14},{2,4},{3,12},{4,2},{5,10},{6,0},{7,8},{9,15},{8,7},{1... | collective-permute-start | bytes 73736 | tf_op jit(solution)/shard_map/ppermute | solution.py:134
  33.6 1.9 %collective-permute-done.5 = bf16[16,768]{1,0:T(8,128)(2,1)S(1)} collective-permute-done((bf16[16,768]{1,0:T(8,128)(2,1)S(1)}, bf16[16,768]{1,0:T(8,128)(2,1)S(1)}, u32[]{:S(2)}, u32[]{:S(2)}) %collective-permute-start.5) | collective-permute-done | bytes 24608 | tf_op jit(solution)/shard_map/ppermute | solution.py:134
  35.5 1.2 %collective-permute-done.7 = bf16[16,768]{1,0:T(8,128)(2,1)S(1)} collective-permute-done((bf16[16,768]{1,0:T(8,128)(2,1)S(1)}, bf16[16,768]{1,0:T(8,128)(2,1)S(1)}, u32[]{:S(2)}, u32[]{:S(2)}) %collective-permute-start.7) | collective-permute-done | bytes 24608 | tf_op jit(solution)/shard_map/ppermute | solution.py:134
  37.4 3.1 %fusion.30 = (bf16[16,768]{1,0:T(8,128)(2,1)S(1)}, f32[16,768]{1,0:T(8,128)S(1)}) fusion(bf16[16,3072]{1,0:T(8,128)(2,1)S(1)} %bitcast.91, bf16[3072,768]{1,0:T(8,128)(2,1)} %param.13), kind=kOutput, calls=%fused_computation.64 | convolution fusion | flops 75509760 | bytes 4890624 | tf_op jit(solution)/shard_map/dot_general | solution.py:17
  40.5 3.7 %collective-permute-start.8 = (bf16[16,768]{1,0:T(8,128)(2,1)S(1)}, bf16[16,768]{1,0:T(8,128)(2,1)S(1)}, u32[]{:S(2)}, u32[]{:S(2)}) collective-permute-start(bf16[16,768]{1,0:T(8,128)(2,1)S(1)} %get-tuple-element.18), channel_id=1, source_target_pairs={{0,1},{1,0},{2,3},{3,2},{4,5},{5,4},{6,7},{7,6},{8,9},{9,8},{10,11... | collective-permute-start | bytes 73736 | tf_op jit(solution)/shard_map/ppermute | solution.py:113
  45.7 0.9 collective-permute-start.12
  46.7 2.2 %collective-permute-start.11 = (bf16[16,768]{1,0:T(8,128)(2,1)S(1)}, bf16[16,768]{1,0:T(8,128)(2,1)S(1)}, u32[]{:S(2)}, u32[]{:S(2)}) collective-permute-start(bf16[16,768]{1,0:T(8,128)(2,1)S(1)} %add_convert_fusion), channel_id=1, source_target_pairs={{0,4},{1,12},{2,6},{3,14},{4,0},{5,8},{6,2},{7,10},{9,13},{8,5},{1... | collective-permute-start | bytes 73736 | tf_op jit(solution)/shard_map/ppermute | solution.py:134
  49.3 1.2 %collective-permute-done.12 = bf16[16,768]{1,0:T(8,128)(2,1)S(1)} collective-permute-done((bf16[16,768]{1,0:T(8,128)(2,1)S(1)}, bf16[16,768]{1,0:T(8,128)(2,1)S(1)}, u32[]{:S(2)}, u32[]{:S(2)}) %collective-permute-start.12) | collective-permute-done | bytes 24608 | tf_op jit(solution)/shard_map/ppermute | solution.py:134
  51.0 1.8 %collective-permute-done.10 = bf16[16,768]{1,0:T(8,128)(2,1)S(1)} collective-permute-done((bf16[16,768]{1,0:T(8,128)(2,1)S(1)}, bf16[16,768]{1,0:T(8,128)(2,1)S(1)}, u32[]{:S(2)}, u32[]{:S(2)}) %collective-permute-start.10) | collective-permute-done | bytes 24608 | tf_op jit(solution)/shard_map/ppermute | solution.py:134
  54.0 4.7 %collective-permute-start.14 = (f32[16,1]{0,1:T(1,128)S(1)}, f32[16,1]{0,1:T(1,128)S(1)}, u32[]{:S(2)}, u32[]{:S(2)}) collective-permute-start(f32[16,1]{0,1:T(1,128)S(1)} %broadcast_in_dim.27), channel_id=1, source_target_pairs={{0,1},{1,0},{2,3},{3,2},{4,5},{5,4},{6,7},{7,6},{8,9},{9,8},{10,11... | collective-permute-start | bytes 200 | tf_op jit(solution)/shard_map/ppermute | solution.py:113
  58.8 7.8 %fusion.17 = f32[16,3072]{1,0:T(8,128)S(1)} fusion(bf16[3072,3072]{1,0:T(8,128)(2,1)} %param.16, f32[16,3072]{1,0:T(8,128)S(1)} %add.48, f32[3072]{0:T(1024)S(1)} %copy-done), kind=kOutput, calls=%fused_computation.38 | convolution fusion | flops 302088192 | bytes 19279872 | tf_op jit(solution)/shard_map/dot_general | solution.py:17
  66.6 8.5 %fusion.18 = f32[16,3072]{1,0:T(8,128)S(1)} fusion(bf16[3072,3072]{1,0:T(8,128)(2,1)} %param.15, f32[16,3072]{1,0:T(8,128)S(1)} %add.48, f32[3072]{0:T(1024)S(1)} %copy-done), kind=kOutput, calls=%fused_computation.39 | convolution fusion | flops 302088192 | bytes 19279872 | tf_op jit(solution)/shard_map/dot_general | solution.py:17
  75.4 1.4 %collective-permute-done.13 = bf16[2,16,3072]{2,1,0:T(8,128)(2,1)S(1)} collective-permute-done((bf16[2,16,3072]{2,1,0:T(8,128)(2,1)S(1)}, bf16[2,16,3072]{2,1,0:T(8,128)(2,1)S(1)}, u32[]{:S(2)}, u32[]{:S(2)}) %collective-permute-start.13) | collective-permute-done | bytes 196640 | tf_op jit(solution)/shard_map/ppermute | solution.py:113
  76.8 2.6 %fusion.10 = f32[16,3072]{1,0:T(8,128)S(1)} fusion(bf16[3072,3072]{1,0:T(8,128)(2,1)S(1)} %bitcast.89, f32[16,3072]{1,0:T(8,128)S(1)} %fusion.17, f32[2,16,3072]{2,1,0:T(8,128)S(1)} %convert_element_type.86, f32[16,3072]{1,0:T(8,128)S(1)} %fusion.18, f32[16]{0:T(128)S(1)} %rsqrt_bitcast_fusion), kind=kOutput, calls=%fused_computation.24 | convolution fusion | flops 302481408 | bytes 19857472 | tf_op jit(solution)/shard_map/dot_general | solution.py:17
  80.2 3.5 %all-to-all-start.1 = ((f32[8,2,3072]{2,1,0:T(2,128)}), f32[8,2,3072]{2,1,0:T(2,128)S(1)}, u32[]{:S(2)}, u32[]{:S(2)}) async-start(f32[8,2,3072]{2,1,0:T(2,128)} %reshape.44), calls=%async_computation.1 | async-start | bytes 393216 | tf_op jit(solution)/shard_map/all_to_all | solution.py:192
  83.7 8.5 %all-to-all-done.1 = f32[8,2,3072]{2,1,0:T(2,128)S(1)} async-done(((f32[8,2,3072]{2,1,0:T(2,128)}), f32[8,2,3072]{2,1,0:T(2,128)S(1)}, u32[]{:S(2)}, u32[]{:S(2)}) %all-to-all-start.1) | async-done | bytes 196640 | tf_op jit(solution)/shard_map/all_to_all | solution.py:192
  (67 shorter events, 8.8 us)
Async XLA Ops:
  0.0 58.8 %copy-start = (f32[3072]{0:T(1024)S(1)}, f32[3072]{0:T(1024)}, u32[]{:S(2)}) copy-start(f32[3072]{0:T(1024)} %param.14) | copy-start | bytes 36868
  1.4 14.4 %all-to-all-start = ((bf16[8,2,3072]{2,1,0:T(2,128)(2,1)}), bf16[8,2,3072]{2,1,0:T(2,128)(2,1)S(1)}, u32[]{:S(2)}, u32[]{:S(2)}) async-start(bf16[8,2,3072]{2,1,0:T(2,128)(2,1)} %broadcast_in_dim.15), calls=%async_computation | async-start | bytes 196608 | tf_op jit(solution)/shard_map/all_to_all | solution.py:109
  16.1 7.5 %collective-permute-start.1 = (f32[16,1]{0,1:T(1,128)S(1)}, f32[16,1]{0,1:T(1,128)S(1)}, u32[]{:S(2)}, u32[]{:S(2)}) collective-permute-start(f32[16,1]{0,1:T(1,128)S(1)} %broadcast_in_dim.26), channel_id=1, source_target_pairs={{0,1},{1,0},{2,3},{3,2},{4,5},{5,4},{6,7},{7,6},{8,9},{9,8},{10,11... | collective-permute-start | bytes 200 | tf_op jit(solution)/shard_map/ppermute | solution.py:113
  23.1 1.4 %collective-permute-start = (bf16[16,2304]{1,0:T(8,128)(2,1)S(1)}, bf16[16,2304]{1,0:T(8,128)(2,1)S(1)}, u32[]{:S(2)}, u32[]{:S(2)}) collective-permute-start(bf16[16,2304]{1,0:T(8,128)(2,1)S(1)} %get-tuple-element.14), channel_id=1, source_target_pairs={{0,1},{1,0},{2,3},{3,2},{4,5},{5,4},{6,7},{7,6},{8,9},{9,8},{10,11... | collective-permute-start | bytes 221192 | tf_op jit(solution)/shard_map/ppermute | solution.py:113
  24.6 3.9 %collective-permute-start.3 = (bf16[16,768]{1,0:T(8,128)(2,1)S(1)}, bf16[16,768]{1,0:T(8,128)(2,1)S(1)}, u32[]{:S(2)}, u32[]{:S(2)}) collective-permute-start(bf16[16,768]{1,0:T(8,128)(2,1)S(1)} %get-tuple-element.10), channel_id=1, source_target_pairs={{0,4},{2,6},{4,0},{6,2},{8,12},{10,14},{12,8},{14,10},{1,5},{3,7},... | collective-permute-start | bytes 73736 | tf_op jit(solution)/shard_map/ppermute | solution.py:164
  24.7 3.9 %collective-permute-start.2 = (bf16[16,768]{1,0:T(8,128)(2,1)S(1)}, bf16[16,768]{1,0:T(8,128)(2,1)S(1)}, u32[]{:S(2)}, u32[]{:S(2)}) collective-permute-start(bf16[16,768]{1,0:T(8,128)(2,1)S(1)} %get-tuple-element.11), channel_id=1, source_target_pairs={{0,2},{2,0},{4,6},{6,4},{8,10},{10,8},{12,14},{14,12},{1,3},{3,1},... | collective-permute-start | bytes 73736 | tf_op jit(solution)/shard_map/ppermute | solution.py:163
  29.0 4.3 %collective-permute-start.4 = (bf16[16,768]{1,0:T(8,128)(2,1)S(1)}, bf16[16,768]{1,0:T(8,128)(2,1)S(1)}, u32[]{:S(2)}, u32[]{:S(2)}) collective-permute-start(bf16[16,768]{1,0:T(8,128)(2,1)S(1)} %bitcast.98), channel_id=1, source_target_pairs={{1,8},{3,10},{5,12},{7,14},{8,1},{10,3},{12,5},{14,7},{17,24},{19,... | collective-permute-start | bytes 73736 | tf_op jit(solution)/shard_map/ppermute | solution.py:134
  29.7 3.9 %collective-permute-start.6 = (bf16[16,768]{1,0:T(8,128)(2,1)S(1)}, bf16[16,768]{1,0:T(8,128)(2,1)S(1)}, u32[]{:S(2)}, u32[]{:S(2)}) collective-permute-start(bf16[16,768]{1,0:T(8,128)(2,1)S(1)} %bitcast.99), channel_id=1, source_target_pairs={{0,4},{1,12},{2,6},{3,14},{4,0},{5,8},{6,2},{7,10},{9,13},{8,5},{1... | collective-permute-start | bytes 73736 | tf_op jit(solution)/shard_map/ppermute | solution.py:134
  31.7 3.8 %collective-permute-start.5 = (bf16[16,768]{1,0:T(8,128)(2,1)S(1)}, bf16[16,768]{1,0:T(8,128)(2,1)S(1)}, u32[]{:S(2)}, u32[]{:S(2)}) collective-permute-start(bf16[16,768]{1,0:T(8,128)(2,1)S(1)} %bitcast.100), channel_id=1, source_target_pairs={{0,2},{1,10},{2,0},{3,8},{4,6},{5,14},{6,4},{7,12},{9,11},{8,3},{1... | collective-permute-start | bytes 73736 | tf_op jit(solution)/shard_map/ppermute | solution.py:134
  32.0 4.7 %collective-permute-start.7 = (bf16[16,768]{1,0:T(8,128)(2,1)S(1)}, bf16[16,768]{1,0:T(8,128)(2,1)S(1)}, u32[]{:S(2)}, u32[]{:S(2)}) collective-permute-start(bf16[16,768]{1,0:T(8,128)(2,1)S(1)} %bitcast.101), channel_id=1, source_target_pairs={{0,6},{1,14},{2,4},{3,12},{4,2},{5,10},{6,0},{7,8},{9,15},{8,7},{1... | collective-permute-start | bytes 73736 | tf_op jit(solution)/shard_map/ppermute | solution.py:134
  40.5 4.6 %collective-permute-start.8 = (bf16[16,768]{1,0:T(8,128)(2,1)S(1)}, bf16[16,768]{1,0:T(8,128)(2,1)S(1)}, u32[]{:S(2)}, u32[]{:S(2)}) collective-permute-start(bf16[16,768]{1,0:T(8,128)(2,1)S(1)} %get-tuple-element.18), channel_id=1, source_target_pairs={{0,1},{1,0},{2,3},{3,2},{4,5},{5,4},{6,7},{7,6},{8,9},{9,8},{10,11... | collective-permute-start | bytes 73736 | tf_op jit(solution)/shard_map/ppermute | solution.py:113
  45.1 4.2 %collective-permute-start.9 = (bf16[16,768]{1,0:T(8,128)(2,1)S(1)}, bf16[16,768]{1,0:T(8,128)(2,1)S(1)}, u32[]{:S(2)}, u32[]{:S(2)}) collective-permute-start(bf16[16,768]{1,0:T(8,128)(2,1)S(1)} %add_convert_fusion), channel_id=1, source_target_pairs={{1,8},{3,10},{5,12},{7,14},{8,1},{10,3},{12,5},{14,7},{17,24},{19,... | collective-permute-start | bytes 73736 | tf_op jit(solution)/shard_map/ppermute | solution.py:134
  45.7 4.8 %collective-permute-start.12 = (bf16[16,768]{1,0:T(8,128)(2,1)S(1)}, bf16[16,768]{1,0:T(8,128)(2,1)S(1)}, u32[]{:S(2)}, u32[]{:S(2)}) collective-permute-start(bf16[16,768]{1,0:T(8,128)(2,1)S(1)} %add_convert_fusion), channel_id=1, source_target_pairs={{0,6},{1,14},{2,4},{3,12},{4,2},{5,10},{6,0},{7,8},{9,15},{8,7},{1... | collective-permute-start | bytes 73736 | tf_op jit(solution)/shard_map/ppermute | solution.py:134
  46.7 4.3 %collective-permute-start.11 = (bf16[16,768]{1,0:T(8,128)(2,1)S(1)}, bf16[16,768]{1,0:T(8,128)(2,1)S(1)}, u32[]{:S(2)}, u32[]{:S(2)}) collective-permute-start(bf16[16,768]{1,0:T(8,128)(2,1)S(1)} %add_convert_fusion), channel_id=1, source_target_pairs={{0,4},{1,12},{2,6},{3,14},{4,0},{5,8},{6,2},{7,10},{9,13},{8,5},{1... | collective-permute-start | bytes 73736 | tf_op jit(solution)/shard_map/ppermute | solution.py:134
  48.9 3.8 %collective-permute-start.10 = (bf16[16,768]{1,0:T(8,128)(2,1)S(1)}, bf16[16,768]{1,0:T(8,128)(2,1)S(1)}, u32[]{:S(2)}, u32[]{:S(2)}) collective-permute-start(bf16[16,768]{1,0:T(8,128)(2,1)S(1)} %add_convert_fusion), channel_id=1, source_target_pairs={{0,2},{1,10},{2,0},{3,8},{4,6},{5,14},{6,4},{7,12},{9,11},{8,3},{1... | collective-permute-start | bytes 73736 | tf_op jit(solution)/shard_map/ppermute | solution.py:134
  54.0 21.3 %collective-permute-start.14 = (f32[16,1]{0,1:T(1,128)S(1)}, f32[16,1]{0,1:T(1,128)S(1)}, u32[]{:S(2)}, u32[]{:S(2)}) collective-permute-start(f32[16,1]{0,1:T(1,128)S(1)} %broadcast_in_dim.27), channel_id=1, source_target_pairs={{0,1},{1,0},{2,3},{3,2},{4,5},{5,4},{6,7},{7,6},{8,9},{9,8},{10,11... | collective-permute-start | bytes 200 | tf_op jit(solution)/shard_map/ppermute | solution.py:113
  58.8 18.0 %slice-start = ((s8[18874368]{0:T(1024)(128)(4,1)}), s8[4194304]{0:T(1024)(128)(4,1)S(1)}, s32[]{:S(2)}) async-start(s8[18874368]{0:T(1024)(128)(4,1)} %bitcast.88), calls=%async_computation.2 | async-start | bytes 8388608
  58.8 18.0 %slice-start.1 = ((s8[18874368]{0:T(1024)(128)(4,1)}), s8[4194304]{0:T(1024)(128)(4,1)S(1)}, s32[]{:S(2)}) async-start(s8[18874368]{0:T(1024)(128)(4,1)} %bitcast.88), calls=%async_computation.3 | async-start | bytes 8388608
  58.8 18.0 %slice-start.2 = ((s8[18874368]{0:T(1024)(128)(4,1)}), s8[4194304]{0:T(1024)(128)(4,1)S(1)}, s32[]{:S(2)}) async-start(s8[18874368]{0:T(1024)(128)(4,1)} %bitcast.88), calls=%async_computation.4 | async-start | bytes 8388608
  66.6 10.2 %slice-start.3 = ((s8[18874368]{0:T(1024)(128)(4,1)}), s8[4194304]{0:T(1024)(128)(4,1)S(1)}, s32[]{:S(2)}) async-start(s8[18874368]{0:T(1024)(128)(4,1)} %bitcast.88), calls=%async_computation.5 | async-start | bytes 8388608
  66.6 10.2 %slice-start.4 = ((s8[18874368]{0:T(1024)(128)(4,1)}), s8[2097152]{0:T(1024)(128)(4,1)S(1)}, s32[]{:S(2)}) async-start(s8[18874368]{0:T(1024)(128)(4,1)} %bitcast.88), calls=%async_computation.6 | async-start | bytes 4194304
  75.3 1.5 %collective-permute-start.13 = (bf16[2,16,3072]{2,1,0:T(8,128)(2,1)S(1)}, bf16[2,16,3072]{2,1,0:T(8,128)(2,1)S(1)}, u32[]{:S(2)}, u32[]{:S(2)}) collective-permute-start(bf16[2,16,3072]{2,1,0:T(8,128)(2,1)S(1)} %pad_maximum_fusion), channel_id=1, source_target_pairs={{0,1},{1,0},{2,3},{3,2},{4,5},{5,4},{6,7},{7,6},{8,9},{9,8},{10,11... | collective-permute-start | bytes 589832 | tf_op jit(solution)/shard_map/ppermute | solution.py:113
  80.2 12.0 %all-to-all-start.1 = ((f32[8,2,3072]{2,1,0:T(2,128)}), f32[8,2,3072]{2,1,0:T(2,128)S(1)}, u32[]{:S(2)}, u32[]{:S(2)}) async-start(f32[8,2,3072]{2,1,0:T(2,128)} %reshape.44), calls=%async_computation.1 | async-start | bytes 393216 | tf_op jit(solution)/shard_map/all_to_all | solution.py:192

commit v2 on v0

--- a/solution.py
+++ b/solution.py
@@ -1,8 +1,11 @@
+import functools
 import math
 
 import jax
 import jax.numpy as jnp
 from jax import lax
+from jax.experimental import pallas as pl
+from jax.experimental.pallas import tpu as pltpu
 from jax.sharding import PartitionSpec as P
 
 HEADS = 48
@@ -103,9 +106,248 @@
     return (resid + lowered).astype(jnp.bfloat16)
 
 
+SQUARE = 4
+MIB = 2**20
+
+
+def call(kernel, outs, *arrays, scratch=(), flops=2 * 10**9):
+    whole = pl.BlockSpec(memory_space=pltpu.VMEM)
+    return pl.pallas_call(
+        kernel,
+        out_shape=[jax.ShapeDtypeStruct(*out) for out in outs],
+        in_specs=[whole] * len(arrays),
+        out_specs=[whole] * len(outs),
+        scratch_shapes=list(scratch),
+        cost_estimate=pl.CostEstimate(flops=flops, bytes_accessed=10**5, transcendentals=0),
+        compiler_params=pltpu.CompilerParams(vmem_limit_bytes=2 * MIB),
+    )(*arrays)
+
+
+def other_core(block):
+    return lax.ppermute(block, "col", [(0, 1), (1, 0)])
+
+
+def from_row(block, step):
+    count = lax.axis_size("row")
+    return lax.ppermute(block, "row", [(i, i ^ step) for i in range(count)])
+
+
+def spread(block):
+    got = []
+    for step in range(SQUARE):
+        pairs = []
+        for chip in range(lax.axis_size("row")):
+            square, place = chip // SQUARE, chip % SQUARE
+            if step > 0:
+                pairs.append((2 * chip + square, 2 * (SQUARE * square + (place ^ step)) + square))
+            away = 1 - square
+            pairs.append((2 * chip + away, 2 * (SQUARE * away + (place ^ step)) + square))
+        got.append(lax.ppermute(block, ("row", "col"), pairs))
+    return got
+
+
+def at_home():
+    return lax.axis_index("row") // SQUARE == lax.axis_index("col")
+
+
+def lanes(values):
+    return jnp.broadcast_to(values, (values.shape[0], 128))
+
+
+def pair_kernel(mine_ref, other_ref, both_ref):
+    both_ref[0] = mine_ref[...]
+    both_ref[1] = other_ref[...]
+
+
+def enter_kernel(*refs):
+    pairs, (scale_ref, stream_ref, scaled_ref, squares_ref, blocks) = refs[:4], refs[4:]
+    mine = lax.axis_index("row")
+    for step, pair_ref in enumerate(pairs):
+        for near in range(2):
+            blocks[mine ^ (2 * step + near)] = pair_ref[near].astype(jnp.float32)
+    count, rows, _ = blocks.shape
+    for block in range(count):
+        stream_ref[rows * block : rows * (block + 1)] = blocks[block]
+    stream = stream_ref[...]
+    scaled_ref[...] = (stream * scale_ref[...][None, :]).astype(jnp.bfloat16)
+    squares_ref[...] = lanes(jnp.sum(stream * stream, axis=-1, keepdims=True))
+
+
+def product_kernel(columns, left_ref, weight_ref, part_ref, sent_ref):
+    for start in range(0, weight_ref.shape[1], columns):
+        at = slice(start, start + columns)
+        part = jnp.dot(left_ref[...], weight_ref[:, at], preferred_element_type=jnp.float32)
+        part_ref[:, at] = part
+        sent_ref[:, at] = part.astype(jnp.bfloat16)
+
+
+def factor(squares_ref, other_ref):
+    total = squares_ref[...] + other_ref[...]
+    return lax.rsqrt(total[:, :1] / D + EPSILON)
+
+
+def units_kernel(part_ref, other_ref, squares_ref, squares_other_ref, kept_ref, near_ref, far_ref):
+    inverse = factor(squares_ref, squares_other_ref)
+    summed = ((part_ref[...] + other_ref[...].astype(jnp.float32)) * inverse).astype(jnp.bfloat16)
+    unit = kept_ref.shape[1]
+    odd = lax.rem(lax.axis_index("row"), 2) == 1
+    first, last = summed[:, :unit], summed[:, 2 * unit :]
+    near_ref[...] = summed[:, unit : 2 * unit]
+
+    @pl.when(odd)
+    def _():
+        kept_ref[...] = last
+        far_ref[...] = first
+
+    @pl.when(jnp.logical_not(odd))
+    def _():
+        kept_ref[...] = first
+        far_ref[...] = last
+
+
+def attend_kernel(kept_ref, near_ref, far_ref, attended_ref, chosen):
+    place = lax.rem(lax.axis_index("row"), SQUARE)
+    query, key, value = 0, 1, 2
+    roles = [(query, key, value), (key, query, value), (key, value, query), (value, key, query)]
+    for at in range(SQUARE):
+
+        @pl.when(place == at)
+        def _(at=at):
+            for role, ref in zip(roles[at], (kept_ref, near_ref, far_ref)):
+                chosen[role] = ref[...]
+
+    for start in range(0, kept_ref.shape[1], HS):
+        head = slice(start, start + HS)
+        scores = lax.dot_general(
+            chosen[query, :, head], chosen[key, :, head], (((1,), (1,)), ((), ())), preferred_element_type=jnp.float32
+        ) * (1.0 / math.sqrt(HS))
+        weights = jnp.exp(scores - jnp.max(scores, axis=-1, keepdims=True))
+        mass = jnp.sum(weights, axis=-1, keepdims=True)
+        mixed = jnp.dot(weights.astype(jnp.bfloat16), chosen[value, :, head], preferred_element_type=jnp.float32)
+        attended_ref[:, head] = (mixed / mass).astype(jnp.bfloat16)
+
+
+def out_kernel(own_ref, *refs):
+    got, (weight_ref, part_ref, sent_ref, blocks) = refs[:SQUARE], refs[SQUARE:]
+    unit = own_ref.shape[1]
+    place = lax.rem(lax.axis_index("row"), SQUARE)
+    blocks[...] = jnp.where(at_home(), own_ref[...], got[0][...])
+    part = None
+    for step in range(SQUARE):
+        left = blocks[...] if step == 0 else got[step][...]
+        rows = pl.ds(pl.multiple_of((place ^ step) * unit, 128), unit)
+        term = jnp.dot(left, weight_ref[rows, :], preferred_element_type=jnp.float32)
+        part = term if part is None else part + term
+    part_ref[...] = part
+    sent_ref[...] = part.astype(jnp.bfloat16)
+
+
+def sum_kernel(part_ref, other_ref, summed_ref):
+    summed_ref[...] = (part_ref[...] + other_ref[...].astype(jnp.float32)).astype(jnp.bfloat16)
+
+
+def resid_kernel(own_ref, *refs):
+    got, (stream_ref, scale_ref, scaled_ref, squares_ref, tokens_ref, resid, blocks) = refs[:SQUARE], refs[SQUARE:]
+    unit = own_ref.shape[1]
+    place = lax.rem(lax.axis_index("row"), SQUARE)
+    for step in range(SQUARE):
+        added = got[step][...]
+        if step == 0:
+            added = jnp.where(at_home(), own_ref[...], added)
+        columns = pl.ds(pl.multiple_of((place ^ step) * unit, 128), unit)
+        resid[:, columns] = stream_ref[:, columns] + added.astype(jnp.float32)
+    whole = resid[...]
+    scaled_ref[...] = (whole * scale_ref[...][None, :]).astype(jnp.bfloat16)
+    squares_ref[...] = lanes(jnp.sum(whole * whole, axis=-1, keepdims=True))
+    count, rows, _ = blocks.shape
+    for block in range(count):
+        blocks[block] = whole[rows * block : rows * (block + 1)]
+    tokens_ref[...] = blocks[lax.axis_index("row")]
+
+
+def down_kernel(columns, *refs):
+    gate_ref, gate_other_ref, up_ref, up_other_ref, squares_ref, squares_other_ref, weight_ref, blocks_ref, hidden = refs
+    inverse = factor(squares_ref, squares_other_ref)
+    gate = (gate_ref[...] + gate_other_ref[...].astype(jnp.float32)) * inverse
+    upward = (up_ref[...] + up_other_ref[...].astype(jnp.float32)) * inverse
+    hidden[...] = (gate / (1.0 + jnp.exp(-gate)) * upward).astype(jnp.bfloat16)
+    count, rows, _ = blocks_ref.shape
+    for start in range(0, weight_ref.shape[1], columns):
+        at = slice(start, start + columns)
+        lowered = jnp.dot(hidden[...], weight_ref[:, at], preferred_element_type=jnp.float32)
+        for block in range(count):
+            blocks_ref[block, :, at] = lowered[rows * block : rows * (block + 1)]
+
+
+def leave_kernel(tokens_ref, blocks_ref, updated_ref):
+    total = tokens_ref[...]
+    for block in range(blocks_ref.shape[0]):
+        total = total + blocks_ref[block]
+    updated_ref[...] = total.astype(jnp.bfloat16)
+
+
+def few_rows(hidden_states, scale_attn, w_qkv, w_out, scale_mlp, w_gate, w_up, w_down):
+    bf16, f32 = jnp.bfloat16, jnp.float32
+    tok_rows, half = hidden_states.shape
+    count = lax.axis_size("row")
+    tokens = tok_rows * count
+
+    [pair] = call(pair_kernel, [((2, tok_rows, half), bf16)], hidden_states, from_row(hidden_states, 1))
+    pairs = [pair] + [from_row(pair, 2 * step) for step in range(1, count // 2)]
+    stream, scaled, squares = call(
+        enter_kernel,
+        [((tokens, half), f32), ((tokens, half), bf16), ((tokens, 128), f32)],
+        *pairs, scale_attn,
+        scratch=[pltpu.VMEM((count, tok_rows, half), f32)],
+    )
+    squares_other = other_core(squares)
+    columns = w_qkv.shape[1]
+    part, sent = call(functools.partial(product_kernel, 256), [((tokens, columns), f32), ((tokens, columns), bf16)], scaled, w_qkv)
+    unit = columns // 3
+    block = ((tokens, unit), bf16)
+    kept, near, far = call(units_kernel, [block] * 3, part, other_core(sent), squares, squares_other)
+    [attended] = call(
+        attend_kernel, [block], kept, from_row(near, 1), from_row(far, 2), scratch=[pltpu.VMEM((3, tokens, unit), bf16)]
+    )
+    part, sent = call(
+        out_kernel,
+        [((tokens, unit), f32), block],
+        attended, *spread(attended), w_out,
+        scratch=[pltpu.VMEM((tokens, unit), bf16)],
+    )
+    [attn_out] = call(sum_kernel, [block], part, other_core(sent))
+    scaled, squares, own = call(
+        resid_kernel,
+        [((tokens, half), bf16), ((tokens, 128), f32), ((tok_rows, half), f32)],
+        attn_out, *spread(attn_out), stream, scale_mlp,
+        scratch=[pltpu.VMEM((tokens, half), f32), pltpu.VMEM((count, tok_rows, half), f32)],
+    )
+    squares_other = other_core(squares)
+    units = w_gate.shape[1]
+    product = functools.partial(product_kernel, 256)
+    parts = [((tokens, units), f32), ((tokens, units), bf16)]
+    gate, gate_sent = call(product, parts, scaled, w_gate)
+    gate_other = other_core(gate_sent)
+    upward, up_sent = call(product, parts, scaled, w_up)
+    [lowered] = call(
+        functools.partial(down_kernel, 256),
+        [((count, tok_rows, half), f32)],
+        gate, gate_other, upward, other_core(up_sent), squares, squares_other, w_down,
+        scratch=[pltpu.VMEM((tokens, units), bf16)],
+    )
+    lowered = lax.all_to_all(lowered, "row", split_axis=0, concat_axis=0, tiled=True)
+    [updated] = call(leave_kernel, [((tok_rows, half), bf16)], own, lowered)
+    return updated
+
+
+def body(*arrays):
+    fits = lax.axis_size("col") == 2 and lax.axis_size("row") == 2 * SQUARE and HEADS % (2 * SQUARE) == 0
+    return (few_rows if fits else per_device)(*arrays)
+
+
 def solution(mesh):
     return jax.shard_map(
-        per_device,
+        body,
         mesh=mesh,
         in_specs=(
             P(("groups", "row"), "col"),

time: 347 us -> 72.5 us (0.21)
  blocking collectives: 193 us -> 12.2 us
  waiting for transfers between devices: 88.5 us -> 16 us
  matrix products: 37.9 us -> 0 us
  starting transfers between devices: 0.13 us -> 30.2 us
  between operations: 13.9 us -> 0.24 us
  Pallas kernels: 0 us -> 12 us
  other arithmetic: 9.66 us -> 0.01 us
    all_gather x6 -> x0, blocking collectives: 156 us -> none  [the longest x1 32.2 us: per_device(): lax.all_gather(normed, 'row', axis=0, tiled=True)]
    unnamed x5 -> x0, waiting for transfers between devices: 70.2 us -> none
    dot_general x7 -> x0, matrix products: 37.9 us -> none  [the longest x2 10 us: project(): return jnp.dot(section, weight, preferred_element_type=jnp.float32)]
    ppermute x0 -> x20, starting transfers between devices: none -> 30.2 us  [the longest x6 12.5 us: other_core(): return lax.ppermute(block, 'col', [(0, 1), (1, 0)])]
    all_to_all x4 -> x1, blocking collectives: 31.8 us -> 12.2 us  [few_rows(): lax.all_to_all(lowered, 'row', split_axis=0, concat_axis=0, tiled=True)]
    reduce_scatter x3 -> x0, waiting for transfers between devices: 18.3 us -> none  [the longest x2 13.4 us: to_rows(): lax.psum_scatter(ordered.astype(jnp.bfloat16), 'col', scatter_dimension=0...]
    ppermute x0 -> x20, waiting for transfers between devices: none -> 16 us  [the longest x6 9.8 us: from_row(): return lax.ppermute(block, 'row', [(i, i ^ step) for i in range(count)])]
    pallas_call x0 -> x12, Pallas kernels: none -> 12 us  [call(): pl.pallas_call(kernel, out_shape=[jax.ShapeDtypeStruct(*out) for out in o...]
  transfers between devices with their start and end apart: 4 -> 20, of which waited for: 4 -> 12; matrix products, arithmetic and copies ran while one was open for 0% -> 0% of each run, Pallas kernels for 0% -> 4%
where the time goes in v2:
time: 72.5 us; the launch traced here: 72.2 us
  starting transfers between devices  30.2 us (42%)
  waiting for transfers between devices  16 us (22%)
  blocking collectives  12.2 us (17%)
  Pallas kernels  12 us (17%)
  local copies, waits for them, and re-layouts  1.51 us (2%)
    ppermute x6, starting transfers between devices, other_core(): return lax.ppermute(block, 'col', [(0, 1), (1, 0)])  12.5 us
    all_to_all x1, blocking collectives, few_rows(): lax.all_to_all(lowered, 'row', split_axis=0, concat_axis=0, tiled=True)  12.2 us
    pallas_call x12, Pallas kernels, call(): pl.pallas_call(kernel, out_shape=[jax.ShapeDtypeStruct(*out) for out in o...  12 us
    ppermute x6, waiting for transfers between devices, from_row(): return lax.ppermute(block, 'row', [(i, i ^ step) for i in range(count)])  9.8 us
    ppermute x6, starting transfers between devices, from_row(): return lax.ppermute(block, 'row', [(i, i ^ step) for i in range(count)])  9.39 us
    ppermute x8, starting transfers between devices, spread(): got.append(lax.ppermute(block, ('row', 'col'), pairs))  8.4 us
    ppermute x8, waiting for transfers between devices, spread(): got.append(lax.ppermute(block, ('row', 'col'), pairs))  3.34 us
    ppermute x6, waiting for transfers between devices, other_core(): return lax.ppermute(block, 'col', [(0, 1), (1, 0)])  2.83 us
  transfers between devices with their start and end apart: 20, of which 12 were waited for; matrix products, arithmetic and copies ran while one was open for 0% of the time, Pallas kernels for 4%

profile of v2, /device:TPU:0, one launch (start us, length us, event | category | flops | bytes accessed | tf_op | source)
XLA Modules:
  0.0 72.2 jit_solution(10236231663467985787)
XLA Ops:
  0.0 2.9 %collective-permute-start = (bf16[2,3072]{1,0:T(2,128)(2,1)}, bf16[2,3072]{1,0:T(2,128)(2,1)S(1)}, u32[]{:S(2)}, u32[]{:S(2)}) collective-permute-start(bf16[2,3072]{1,0:T(2,128)(2,1)} %mine_ref.1), channel_id=1, source_target_pairs={{0,2},{2,0},{4,6},{6,4},{8,10},{10,8},{12,14},{14,12},{1,3},{3,1},... | collective-permute-start | bytes 36872 | tf_op jit(solution)/shard_map/ppermute | solution.py:132
  2.9 1.9 %collective-permute-done.other_ref = bf16[2,3072]{1,0:T(2,128)(2,1)S(1)} collective-permute-done((bf16[2,3072]{1,0:T(2,128)(2,1)}, bf16[2,3072]{1,0:T(2,128)(2,1)S(1)}, u32[]{:S(2)}, u32[]{:S(2)}) %collective-permute-start) | collective-permute-done | bytes 12320 | tf_op jit(solution)/shard_map/ppermute | solution.py:132
  5.5 4.3 %collective-permute-start.3 = (bf16[2,2,3072]{2,1,0:T(2,128)(2,1)S(1)}, bf16[2,2,3072]{2,1,0:T(2,128)(2,1)S(1)}, u32[]{:S(2)}, u32[]{:S(2)}) collective-permute-start(bf16[2,2,3072]{2,1,0:T(2,128)(2,1)S(1)} %shard_map.82.refs_0_), channel_id=1, source_target_pairs={{0,12},{2,14},{4,8},{6,10},{8,4},{10,6},{12,0},{14,2},{1,13},{3,15... | collective-permute-start | bytes 73736 | tf_op jit(solution)/shard_map/ppermute | solution.py:132
  10.4 1.5 %collective-permute-done.3.refs_3_ = bf16[2,2,3072]{2,1,0:T(2,128)(2,1)S(1)} collective-permute-done((bf16[2,2,3072]{2,1,0:T(2,128)(2,1)S(1)}, bf16[2,2,3072]{2,1,0:T(2,128)(2,1)S(1)}, u32[]{:S(2)}, u32[]{:S(2)}) %collective-permute-start.3) | collective-permute-done | bytes 24608 | tf_op jit(solution)/shard_map/ppermute | solution.py:132
  11.9 2.6 %collective-permute-done.2.refs_2_ = bf16[2,2,3072]{2,1,0:T(2,128)(2,1)S(1)} collective-permute-done((bf16[2,2,3072]{2,1,0:T(2,128)(2,1)S(1)}, bf16[2,2,3072]{2,1,0:T(2,128)(2,1)S(1)}, u32[]{:S(2)}, u32[]{:S(2)}) %collective-permute-start.2) | collective-permute-done | bytes 24608 | tf_op jit(solution)/shard_map/ppermute | solution.py:132
  15.4 1.9 %shard_map.84 = (f32[16,2304]{1,0:T(8,128)S(1)}, bf16[16,2304]{1,0:T(8,128)(2,1)S(1)}) custom-call(bf16[16,3072]{1,0:T(8,128)(2,1)S(1)} %get-tuple-element.22.left_ref, bf16[3072,2304]{1,0:T(8,128)(2,1)S(1)} %copy-done), custom_call_target="tpu_custom_call" | custom-call | flops 2000000000 | bytes 100000 | tf_op jit(solution)/shard_map/pallas_call | solution.py:115
  18.8 1.6 %collective-permute-start.6 = (bf16[16,768]{1,0:T(8,128)(2,1)S(1)}, bf16[16,768]{1,0:T(8,128)(2,1)S(1)}, u32[]{:S(2)}, u32[]{:S(2)}) collective-permute-start(bf16[16,768]{1,0:T(8,128)(2,1)S(1)} %get-tuple-element.27), channel_id=1, source_target_pairs={{0,2},{2,0},{4,6},{6,4},{8,10},{10,8},{12,14},{14,12},{1,3},{3,1},... | collective-permute-start | bytes 73736 | tf_op jit(solution)/shard_map/ppermute | solution.py:132
  20.4 2.3 %collective-permute-done.6.near_ref = bf16[16,768]{1,0:T(8,128)(2,1)S(1)} collective-permute-done((bf16[16,768]{1,0:T(8,128)(2,1)S(1)}, bf16[16,768]{1,0:T(8,128)(2,1)S(1)}, u32[]{:S(2)}, u32[]{:S(2)}) %collective-permute-start.6) | collective-permute-done | bytes 24608 | tf_op jit(solution)/shard_map/ppermute | solution.py:132
  22.7 1.5 %collective-permute-done.7.far_ref = bf16[16,768]{1,0:T(8,128)(2,1)S(1)} collective-permute-done((bf16[16,768]{1,0:T(8,128)(2,1)S(1)}, bf16[16,768]{1,0:T(8,128)(2,1)S(1)}, u32[]{:S(2)}, u32[]{:S(2)}) %collective-permute-start.7) | collective-permute-done | bytes 24608 | tf_op jit(solution)/shard_map/ppermute | solution.py:132
  24.9 2.0 %collective-permute-start.10 = (bf16[16,768]{1,0:T(8,128)(2,1)S(1)}, bf16[16,768]{1,0:T(8,128)(2,1)S(1)}, u32[]{:S(2)}, u32[]{:S(2)}) collective-permute-start(bf16[16,768]{1,0:T(8,128)(2,1)S(1)} %shard_map.86.own_ref), channel_id=1, source_target_pairs={{0,4},{1,12},{2,6},{3,14},{4,0},{5,8},{6,2},{7,10},{9,13},{8,5},{1... | collective-permute-start | bytes 73736 | tf_op jit(solution)/shard_map/ppermute | solution.py:145
  26.9 1.5 %collective-permute-start.9 = (bf16[16,768]{1,0:T(8,128)(2,1)S(1)}, bf16[16,768]{1,0:T(8,128)(2,1)S(1)}, u32[]{:S(2)}, u32[]{:S(2)}) collective-permute-start(bf16[16,768]{1,0:T(8,128)(2,1)S(1)} %shard_map.86.own_ref), channel_id=1, source_target_pairs={{0,2},{1,10},{2,0},{3,8},{4,6},{5,14},{6,4},{7,12},{9,11},{8,3},{1... | collective-permute-start | bytes 73736 | tf_op jit(solution)/shard_map/ppermute | solution.py:145
  29.6 1.1 %collective-permute-done.9.refs_1_ = bf16[16,768]{1,0:T(8,128)(2,1)S(1)} collective-permute-done((bf16[16,768]{1,0:T(8,128)(2,1)S(1)}, bf16[16,768]{1,0:T(8,128)(2,1)S(1)}, u32[]{:S(2)}, u32[]{:S(2)}) %collective-permute-start.9) | collective-permute-done | bytes 24608 | tf_op jit(solution)/shard_map/ppermute | solution.py:145
  31.4 5.0 %collective-permute-start.12 = (bf16[16,768]{1,0:T(8,128)(2,1)S(1)}, bf16[16,768]{1,0:T(8,128)(2,1)S(1)}, u32[]{:S(2)}, u32[]{:S(2)}) collective-permute-start(bf16[16,768]{1,0:T(8,128)(2,1)S(1)} %get-tuple-element.30), channel_id=1, source_target_pairs={{0,1},{1,0},{2,3},{3,2},{4,5},{5,4},{6,7},{7,6},{8,9},{9,8},{10,11... | collective-permute-start | bytes 73736 | tf_op jit(solution)/shard_map/ppermute | solution.py:127
  36.4 0.8 %collective-permute-done.12.other_ref = bf16[16,768]{1,0:T(8,128)(2,1)S(1)} collective-permute-done((bf16[16,768]{1,0:T(8,128)(2,1)S(1)}, bf16[16,768]{1,0:T(8,128)(2,1)S(1)}, u32[]{:S(2)}, u32[]{:S(2)}) %collective-permute-start.12) | collective-permute-done | bytes 24608 | tf_op jit(solution)/shard_map/ppermute | solution.py:127
  37.3 1.8 %collective-permute-start.16 = (bf16[16,768]{1,0:T(8,128)(2,1)S(1)}, bf16[16,768]{1,0:T(8,128)(2,1)S(1)}, u32[]{:S(2)}, u32[]{:S(2)}) collective-permute-start(bf16[16,768]{1,0:T(8,128)(2,1)S(1)} %shard_map.88.own_ref), channel_id=1, source_target_pairs={{0,6},{1,14},{2,4},{3,12},{4,2},{5,10},{6,0},{7,8},{9,15},{8,7},{1... | collective-permute-start | bytes 73736 | tf_op jit(solution)/shard_map/ppermute | solution.py:145
  39.4 1.5 %collective-permute-start.14 = (bf16[16,768]{1,0:T(8,128)(2,1)S(1)}, bf16[16,768]{1,0:T(8,128)(2,1)S(1)}, u32[]{:S(2)}, u32[]{:S(2)}) collective-permute-start(bf16[16,768]{1,0:T(8,128)(2,1)S(1)} %shard_map.88.own_ref), channel_id=1, source_target_pairs={{0,2},{1,10},{2,0},{3,8},{4,6},{5,14},{6,4},{7,12},{9,11},{8,3},{1... | collective-permute-start | bytes 73736 | tf_op jit(solution)/shard_map/ppermute | solution.py:145
  42.1 1.1 %collective-permute-done.15.refs_2_ = bf16[16,768]{1,0:T(8,128)(2,1)S(1)} collective-permute-done((bf16[16,768]{1,0:T(8,128)(2,1)S(1)}, bf16[16,768]{1,0:T(8,128)(2,1)S(1)}, u32[]{:S(2)}, u32[]{:S(2)}) %collective-permute-start.15) | collective-permute-done | bytes 24608 | tf_op jit(solution)/shard_map/ppermute | solution.py:145
  43.4 2.5 %shard_map.91 = (f32[16,3072]{1,0:T(8,128)S(1)}, bf16[16,3072]{1,0:T(8,128)(2,1)S(1)}) custom-call(bf16[16,3072]{1,0:T(8,128)(2,1)S(1)} %get-tuple-element.33.left_ref, bf16[3072,3072]{1,0:T(8,128)(2,1)S(1)} %bitcast.1), custom_call_target="tpu_custom_call" | custom-call | flops 2000000000 | bytes 100000 | tf_op jit(solution)/shard_map/pallas_call | solution.py:115
  46.0 5.0 %collective-permute-start.18 = (bf16[16,3072]{1,0:T(8,128)(2,1)S(1)}, bf16[16,3072]{1,0:T(8,128)(2,1)S(1)}, u32[]{:S(2)}, u32[]{:S(2)}) collective-permute-start(bf16[16,3072]{1,0:T(8,128)(2,1)S(1)} %get-tuple-element.37), channel_id=1, source_target_pairs={{0,1},{1,0},{2,3},{3,2},{4,5},{5,4},{6,7},{7,6},{8,9},{9,8},{10,11... | collective-permute-start | bytes 294920 | tf_op jit(solution)/shard_map/ppermute | solution.py:127
  51.0 2.5 %shard_map.90 = (f32[16,3072]{1,0:T(8,128)S(1)}, bf16[16,3072]{1,0:T(8,128)(2,1)S(1)}) custom-call(bf16[16,3072]{1,0:T(8,128)(2,1)S(1)} %get-tuple-element.33.left_ref, bf16[3072,3072]{1,0:T(8,128)(2,1)S(1)} %bitcast.3), custom_call_target="tpu_custom_call" | custom-call | flops 2000000000 | bytes 100000 | tf_op jit(solution)/shard_map/pallas_call | solution.py:115
  53.6 1.9 %collective-permute-start.17 = (bf16[16,3072]{1,0:T(8,128)(2,1)S(1)}, bf16[16,3072]{1,0:T(8,128)(2,1)S(1)}, u32[]{:S(2)}, u32[]{:S(2)}) collective-permute-start(bf16[16,3072]{1,0:T(8,128)(2,1)S(1)} %get-tuple-element.35), channel_id=1, source_target_pairs={{0,1},{1,0},{2,3},{3,2},{4,5},{5,4},{6,7},{7,6},{8,9},{9,8},{10,11... | collective-permute-start | bytes 294920 | tf_op jit(solution)/shard_map/ppermute | solution.py:127
  55.5 1.1 %collective-permute-done.19.refs_5_ = f32[16,128]{1,0:T(8,128)S(1)} collective-permute-done((f32[16,128]{1,0:T(8,128)S(1)}, f32[16,128]{1,0:T(8,128)S(1)}, u32[]{:S(2)}, u32[]{:S(2)}) %collective-permute-start.19) | collective-permute-done | bytes 8224 | tf_op jit(solution)/shard_map/ppermute | solution.py:127
  56.7 2.6 %shard_map.92 = f32[8,2,3072]{2,1,0:T(2,128)S(1)} custom-call(f32[16,3072]{1,0:T(8,128)S(1)} %get-tuple-element.34.refs_0_, bf16[16,3072]{1,0:T(8,128)(2,1)S(1)} %collective-permute-done.17.refs_1_, f32[16,3072]{1,0:T(8,128)S(1)} %get-tuple-element.36.refs_2_, bf16[16,3072]{1,0:T(8,128)(2,1)S(1)} %collective-permute-done.18.refs_3_, ...), custom_call_target="tpu_custom_call" | custom-call | flops 2000000000 | bytes 100000 | tf_op jit(solution)/shard_map/pallas_call | solution.py:115
  59.3 12.2 %all_to_all.5.blocks_ref = f32[8,2,3072]{2,1,0:T(2,128)S(1)} all-to-all(f32[8,2,3072]{2,1,0:T(2,128)S(1)} %shard_map.92), channel_id=1, replica_groups=mesh['groups'=2,'row'=8,'col'=2] {'row'}, dimensions={0} | all-to-all | bytes 393216 | tf_op jit(solution)/shard_map/all_to_all | solution.py:338
  (75 shorter events, 8.7 us)
Async XLA Ops:
  0.0 4.8 %collective-permute-start = (bf16[2,3072]{1,0:T(2,128)(2,1)}, bf16[2,3072]{1,0:T(2,128)(2,1)S(1)}, u32[]{:S(2)}, u32[]{:S(2)}) collective-permute-start(bf16[2,3072]{1,0:T(2,128)(2,1)} %mine_ref.1), channel_id=1, source_target_pairs={{0,2},{2,0},{4,6},{6,4},{8,10},{10,8},{12,14},{14,12},{1,3},{3,1},... | collective-permute-start | bytes 36872 | tf_op jit(solution)/shard_map/ppermute | solution.py:132
  5.5 6.4 %collective-permute-start.3 = (bf16[2,2,3072]{2,1,0:T(2,128)(2,1)S(1)}, bf16[2,2,3072]{2,1,0:T(2,128)(2,1)S(1)}, u32[]{:S(2)}, u32[]{:S(2)}) collective-permute-start(bf16[2,2,3072]{2,1,0:T(2,128)(2,1)S(1)} %shard_map.82.refs_0_), channel_id=1, source_target_pairs={{0,12},{2,14},{4,8},{6,10},{8,4},{10,6},{12,0},{14,2},{1,13},{3,15... | collective-permute-start | bytes 73736 | tf_op jit(solution)/shard_map/ppermute | solution.py:132
  9.8 4.7 %collective-permute-start.2 = (bf16[2,2,3072]{2,1,0:T(2,128)(2,1)S(1)}, bf16[2,2,3072]{2,1,0:T(2,128)(2,1)S(1)}, u32[]{:S(2)}, u32[]{:S(2)}) collective-permute-start(bf16[2,2,3072]{2,1,0:T(2,128)(2,1)S(1)} %shard_map.82.refs_0_), channel_id=1, source_target_pairs={{0,8},{2,10},{4,12},{6,14},{8,0},{10,2},{12,4},{14,6},{1,9},{3,11}... | collective-permute-start | bytes 73736 | tf_op jit(solution)/shard_map/ppermute | solution.py:132
  9.8 4.7 %collective-permute-start.1 = (bf16[2,2,3072]{2,1,0:T(2,128)(2,1)S(1)}, bf16[2,2,3072]{2,1,0:T(2,128)(2,1)S(1)}, u32[]{:S(2)}, u32[]{:S(2)}) collective-permute-start(bf16[2,2,3072]{2,1,0:T(2,128)(2,1)S(1)} %shard_map.82.refs_0_), channel_id=1, source_target_pairs={{0,4},{2,6},{4,0},{6,2},{8,12},{10,14},{12,8},{14,10},{1,5},{3,7},... | collective-permute-start | bytes 73736 | tf_op jit(solution)/shard_map/ppermute | solution.py:132
  15.4 27.8 %copy-start.3 = (f32[3072]{0:T(1024)S(1)}, f32[3072]{0:T(1024)}, u32[]{:S(2)}) copy-start(f32[3072]{0:T(1024)} %refs_5_.1) | copy-start | bytes 36868
  17.4 26.0 %slice-start = ((s8[18874368]{0:T(1024)(128)(4,1)}), s8[4194304]{0:T(1024)(128)(4,1)S(1)}, s32[]{:S(2)}) async-start(s8[18874368]{0:T(1024)(128)(4,1)} %bitcast), calls=%async_computation.1 | async-start | bytes 8388608
  17.4 1.4 %collective-permute-start.4 = (bf16[16,2304]{1,0:T(8,128)(2,1)S(1)}, bf16[16,2304]{1,0:T(8,128)(2,1)S(1)}, u32[]{:S(2)}, u32[]{:S(2)}) collective-permute-start(bf16[16,2304]{1,0:T(8,128)(2,1)S(1)} %get-tuple-element.24), channel_id=1, source_target_pairs={{0,1},{1,0},{2,3},{3,2},{4,5},{5,4},{6,7},{7,6},{8,9},{9,8},{10,11... | collective-permute-start | bytes 221192 | tf_op jit(solution)/shard_map/ppermute | solution.py:127
  17.4 1.3 %collective-permute-start.5 = (f32[16,128]{1,0:T(8,128)S(1)}, f32[16,128]{1,0:T(8,128)S(1)}, u32[]{:S(2)}, u32[]{:S(2)}) collective-permute-start(f32[16,128]{1,0:T(8,128)S(1)} %get-tuple-element.25.squares_ref), channel_id=1, source_target_pairs={{0,1},{1,0},{2,3},{3,2},{4,5},{5,4},{6,7},{7,6},{8,9},{9,8},{10,11... | collective-permute-start | bytes 24584 | tf_op jit(solution)/shard_map/ppermute | solution.py:127
  18.8 3.9 %collective-permute-start.6 = (bf16[16,768]{1,0:T(8,128)(2,1)S(1)}, bf16[16,768]{1,0:T(8,128)(2,1)S(1)}, u32[]{:S(2)}, u32[]{:S(2)}) collective-permute-start(bf16[16,768]{1,0:T(8,128)(2,1)S(1)} %get-tuple-element.27), channel_id=1, source_target_pairs={{0,2},{2,0},{4,6},{6,4},{8,10},{10,8},{12,14},{14,12},{1,3},{3,1},... | collective-permute-start | bytes 73736 | tf_op jit(solution)/shard_map/ppermute | solution.py:132
  20.4 3.8 %collective-permute-start.7 = (bf16[16,768]{1,0:T(8,128)(2,1)S(1)}, bf16[16,768]{1,0:T(8,128)(2,1)S(1)}, u32[]{:S(2)}, u32[]{:S(2)}) collective-permute-start(bf16[16,768]{1,0:T(8,128)(2,1)S(1)} %get-tuple-element.28), channel_id=1, source_target_pairs={{0,4},{2,6},{4,0},{6,2},{8,12},{10,14},{12,8},{14,10},{1,5},{3,7},... | collective-permute-start | bytes 73736 | tf_op jit(solution)/shard_map/ppermute | solution.py:132
  24.8 26.2 %slice-start.5 = ((s8[18874368]{0:T(1024)(128)(4,1)}), s8[2097152]{0:T(1024)(128)(4,1)S(1)}, s32[]{:S(2)}) async-start(s8[18874368]{0:T(1024)(128)(4,1)} %bitcast.2), calls=%async_computation.6 | async-start | bytes 4194304
  24.8 4.8 %collective-permute-start.11 = (bf16[16,768]{1,0:T(8,128)(2,1)S(1)}, bf16[16,768]{1,0:T(8,128)(2,1)S(1)}, u32[]{:S(2)}, u32[]{:S(2)}) collective-permute-start(bf16[16,768]{1,0:T(8,128)(2,1)S(1)} %shard_map.86.own_ref), channel_id=1, source_target_pairs={{0,6},{1,14},{2,4},{3,12},{4,2},{5,10},{6,0},{7,8},{9,15},{8,7},{1... | collective-permute-start | bytes 73736 | tf_op jit(solution)/shard_map/ppermute | solution.py:145
  24.9 4.7 %collective-permute-start.10 = (bf16[16,768]{1,0:T(8,128)(2,1)S(1)}, bf16[16,768]{1,0:T(8,128)(2,1)S(1)}, u32[]{:S(2)}, u32[]{:S(2)}) collective-permute-start(bf16[16,768]{1,0:T(8,128)(2,1)S(1)} %shard_map.86.own_ref), channel_id=1, source_target_pairs={{0,4},{1,12},{2,6},{3,14},{4,0},{5,8},{6,2},{7,10},{9,13},{8,5},{1... | collective-permute-start | bytes 73736 | tf_op jit(solution)/shard_map/ppermute | solution.py:145
  26.9 3.8 %collective-permute-start.9 = (bf16[16,768]{1,0:T(8,128)(2,1)S(1)}, bf16[16,768]{1,0:T(8,128)(2,1)S(1)}, u32[]{:S(2)}, u32[]{:S(2)}) collective-permute-start(bf16[16,768]{1,0:T(8,128)(2,1)S(1)} %shard_map.86.own_ref), channel_id=1, source_target_pairs={{0,2},{1,10},{2,0},{3,8},{4,6},{5,14},{6,4},{7,12},{9,11},{8,3},{1... | collective-permute-start | bytes 73736 | tf_op jit(solution)/shard_map/ppermute | solution.py:145
  28.4 2.3 %collective-permute-start.8 = (bf16[16,768]{1,0:T(8,128)(2,1)S(1)}, bf16[16,768]{1,0:T(8,128)(2,1)S(1)}, u32[]{:S(2)}, u32[]{:S(2)}) collective-permute-start(bf16[16,768]{1,0:T(8,128)(2,1)S(1)} %shard_map.86.own_ref), channel_id=1, source_target_pairs={{1,8},{3,10},{5,12},{7,14},{8,1},{10,3},{12,5},{14,7},{17,24},{19,... | collective-permute-start | bytes 73736 | tf_op jit(solution)/shard_map/ppermute | solution.py:145
  30.7 26.0 %slice-start.10 = ((s8[18874368]{0:T(1024)(128)(4,1)}), s8[2097152]{0:T(1024)(128)(4,1)S(1)}, s32[]{:S(2)}) async-start(s8[18874368]{0:T(1024)(128)(4,1)} %bitcast.4), calls=%async_computation.11 | async-start | bytes 4194304
  31.4 5.8 %collective-permute-start.12 = (bf16[16,768]{1,0:T(8,128)(2,1)S(1)}, bf16[16,768]{1,0:T(8,128)(2,1)S(1)}, u32[]{:S(2)}, u32[]{:S(2)}) collective-permute-start(bf16[16,768]{1,0:T(8,128)(2,1)S(1)} %get-tuple-element.30), channel_id=1, source_target_pairs={{0,1},{1,0},{2,3},{3,2},{4,5},{5,4},{6,7},{7,6},{8,9},{9,8},{10,11... | collective-permute-start | bytes 73736 | tf_op jit(solution)/shard_map/ppermute | solution.py:127
  37.3 4.8 %collective-permute-start.16 = (bf16[16,768]{1,0:T(8,128)(2,1)S(1)}, bf16[16,768]{1,0:T(8,128)(2,1)S(1)}, u32[]{:S(2)}, u32[]{:S(2)}) collective-permute-start(bf16[16,768]{1,0:T(8,128)(2,1)S(1)} %shard_map.88.own_ref), channel_id=1, source_target_pairs={{0,6},{1,14},{2,4},{3,12},{4,2},{5,10},{6,0},{7,8},{9,15},{8,7},{1... | collective-permute-start | bytes 73736 | tf_op jit(solution)/shard_map/ppermute | solution.py:145
  39.1 4.0 %collective-permute-start.15 = (bf16[16,768]{1,0:T(8,128)(2,1)S(1)}, bf16[16,768]{1,0:T(8,128)(2,1)S(1)}, u32[]{:S(2)}, u32[]{:S(2)}) collective-permute-start(bf16[16,768]{1,0:T(8,128)(2,1)S(1)} %shard_map.88.own_ref), channel_id=1, source_target_pairs={{0,4},{1,12},{2,6},{3,14},{4,0},{5,8},{6,2},{7,10},{9,13},{8,5},{1... | collective-permute-start | bytes 73736 | tf_op jit(solution)/shard_map/ppermute | solution.py:145
  39.4 3.8 %collective-permute-start.14 = (bf16[16,768]{1,0:T(8,128)(2,1)S(1)}, bf16[16,768]{1,0:T(8,128)(2,1)S(1)}, u32[]{:S(2)}, u32[]{:S(2)}) collective-permute-start(bf16[16,768]{1,0:T(8,128)(2,1)S(1)} %shard_map.88.own_ref), channel_id=1, source_target_pairs={{0,2},{1,10},{2,0},{3,8},{4,6},{5,14},{6,4},{7,12},{9,11},{8,3},{1... | collective-permute-start | bytes 73736 | tf_op jit(solution)/shard_map/ppermute | solution.py:145
  40.9 2.3 %collective-permute-start.13 = (bf16[16,768]{1,0:T(8,128)(2,1)S(1)}, bf16[16,768]{1,0:T(8,128)(2,1)S(1)}, u32[]{:S(2)}, u32[]{:S(2)}) collective-permute-start(bf16[16,768]{1,0:T(8,128)(2,1)S(1)} %shard_map.88.own_ref), channel_id=1, source_target_pairs={{1,8},{3,10},{5,12},{7,14},{8,1},{10,3},{12,5},{14,7},{17,24},{19,... | collective-permute-start | bytes 73736 | tf_op jit(solution)/shard_map/ppermute | solution.py:145
  46.0 10.7 %collective-permute-start.18 = (bf16[16,3072]{1,0:T(8,128)(2,1)S(1)}, bf16[16,3072]{1,0:T(8,128)(2,1)S(1)}, u32[]{:S(2)}, u32[]{:S(2)}) collective-permute-start(bf16[16,3072]{1,0:T(8,128)(2,1)S(1)} %get-tuple-element.37), channel_id=1, source_target_pairs={{0,1},{1,0},{2,3},{3,2},{4,5},{5,4},{6,7},{7,6},{8,9},{9,8},{10,11... | collective-permute-start | bytes 294920 | tf_op jit(solution)/shard_map/ppermute | solution.py:127
  53.6 3.1 %collective-permute-start.17 = (bf16[16,3072]{1,0:T(8,128)(2,1)S(1)}, bf16[16,3072]{1,0:T(8,128)(2,1)S(1)}, u32[]{:S(2)}, u32[]{:S(2)}) collective-permute-start(bf16[16,3072]{1,0:T(8,128)(2,1)S(1)} %get-tuple-element.35), channel_id=1, source_target_pairs={{0,1},{1,0},{2,3},{3,2},{4,5},{5,4},{6,7},{7,6},{8,9},{9,8},{10,11... | collective-permute-start | bytes 294920 | tf_op jit(solution)/shard_map/ppermute | solution.py:127
  55.5 1.2 %collective-permute-start.19 = (f32[16,128]{1,0:T(8,128)S(1)}, f32[16,128]{1,0:T(8,128)S(1)}, u32[]{:S(2)}, u32[]{:S(2)}) collective-permute-start(f32[16,128]{1,0:T(8,128)S(1)} %get-tuple-element.38.refs_4_), channel_id=1, source_target_pairs={{0,1},{1,0},{2,3},{3,2},{4,5},{5,4},{6,7},{7,6},{8,9},{9,8},{10,11... | collective-permute-start | bytes 24584 | tf_op jit(solution)/shard_map/ppermute | solution.py:127
  (17 other events, 219.0 us)

commit v3 on v2

--- a/solution.py
+++ b/solution.py
@@ -119,7 +119,7 @@
         out_specs=[whole] * len(outs),
         scratch_shapes=list(scratch),
         cost_estimate=pl.CostEstimate(flops=flops, bytes_accessed=10**5, transcendentals=0),
-        compiler_params=pltpu.CompilerParams(vmem_limit_bytes=2 * MIB),
+        compiler_params=pltpu.CompilerParams(vmem_limit_bytes=3 * MIB),
     )(*arrays)
 
 
@@ -134,14 +134,13 @@
 
 def spread(block):
     got = []
-    for step in range(SQUARE):
+    for step in range(2):
         pairs = []
         for chip in range(lax.axis_size("row")):
-            square, place = chip // SQUARE, chip % SQUARE
+            square = chip // SQUARE
             if step > 0:
-                pairs.append((2 * chip + square, 2 * (SQUARE * square + (place ^ step)) + square))
-            away = 1 - square
-            pairs.append((2 * chip + away, 2 * (SQUARE * away + (place ^ step)) + square))
+                pairs.append((2 * chip + square, 2 * (chip ^ 2) + square))
+            pairs.append((2 * chip + 1 - square, 2 * (chip ^ SQUARE ^ (2 * step)) + square))
         got.append(lax.ppermute(block, ("row", "col"), pairs))
     return got
 
@@ -150,8 +149,22 @@
     return lax.axis_index("row") // SQUARE == lax.axis_index("col")
 
 
+def pair_place():
+    return lax.rem(lax.axis_index("row"), SQUARE) // 2
+
+
+def arrange(own_ref, got):
+    return jnp.where(at_home(), own_ref[...], got[0][...]), got[1][...]
+
+
 def lanes(values):
     return jnp.broadcast_to(values, (values.shape[0], 128))
+
+
+def bring_kernel(*refs):
+    half = len(refs) // 2
+    for source, target in zip(refs[:half], refs[half:]):
+        target[...] = source[...]
 
 
 def pair_kernel(mine_ref, other_ref, both_ref):
@@ -186,35 +199,38 @@
     return lax.rsqrt(total[:, :1] / D + EPSILON)
 
 
-def units_kernel(part_ref, other_ref, squares_ref, squares_other_ref, kept_ref, near_ref, far_ref):
+def units_kernel(part_ref, other_ref, squares_ref, squares_other_ref, near_ref, far_ref):
     inverse = factor(squares_ref, squares_other_ref)
     summed = ((part_ref[...] + other_ref[...].astype(jnp.float32)) * inverse).astype(jnp.bfloat16)
-    unit = kept_ref.shape[1]
+    unit = far_ref.shape[1]
     odd = lax.rem(lax.axis_index("row"), 2) == 1
-    first, last = summed[:, :unit], summed[:, 2 * unit :]
-    near_ref[...] = summed[:, unit : 2 * unit]
 
     @pl.when(odd)
     def _():
-        kept_ref[...] = last
-        far_ref[...] = first
+        near_ref[...] = summed[:, unit:]
+        far_ref[...] = summed[:, :unit]
 
     @pl.when(jnp.logical_not(odd))
     def _():
-        kept_ref[...] = first
-        far_ref[...] = last
-
-
-def attend_kernel(kept_ref, near_ref, far_ref, attended_ref, chosen):
+        near_ref[...] = summed[:, : 2 * unit]
+        far_ref[...] = summed[:, 2 * unit :]
+
+
+def attend_kernel(kept_ref, near_ref, straight_ref, across_ref, attended_ref, chosen):
     place = lax.rem(lax.axis_index("row"), SQUARE)
+    unit = straight_ref.shape[1]
     query, key, value = 0, 1, 2
     roles = [(query, key, value), (key, query, value), (key, value, query), (value, key, query)]
     for at in range(SQUARE):
 
         @pl.when(place == at)
         def _(at=at):
-            for role, ref in zip(roles[at], (kept_ref, near_ref, far_ref)):
-                chosen[role] = ref[...]
+            kept, near, far = roles[at]
+            chosen[kept] = kept_ref[...]
+            chosen[near] = near_ref[...]
+            first, last = (straight_ref, across_ref) if at % 2 == 0 else (across_ref, straight_ref)
+            chosen[far, :, :unit] = first[...]
+            chosen[far, :, unit:] = last[...]
 
     for start in range(0, kept_ref.shape[1], HS):
         head = slice(start, start + HS)
@@ -228,33 +244,30 @@
 
 
 def out_kernel(own_ref, *refs):
-    got, (weight_ref, part_ref, sent_ref, blocks) = refs[:SQUARE], refs[SQUARE:]
-    unit = own_ref.shape[1]
-    place = lax.rem(lax.axis_index("row"), SQUARE)
-    blocks[...] = jnp.where(at_home(), own_ref[...], got[0][...])
+    got, (weight_ref, part_ref) = refs[:2], refs[2:]
+    width = own_ref.shape[1]
     part = None
-    for step in range(SQUARE):
-        left = blocks[...] if step == 0 else got[step][...]
-        rows = pl.ds(pl.multiple_of((place ^ step) * unit, 128), unit)
+    for step, left in enumerate(arrange(own_ref, got)):
+        rows = pl.ds(pl.multiple_of((pair_place() ^ step) * width, 128), width)
         term = jnp.dot(left, weight_ref[rows, :], preferred_element_type=jnp.float32)
         part = term if part is None else part + term
-    part_ref[...] = part
-    sent_ref[...] = part.astype(jnp.bfloat16)
-
-
-def sum_kernel(part_ref, other_ref, summed_ref):
-    summed_ref[...] = (part_ref[...] + other_ref[...].astype(jnp.float32)).astype(jnp.bfloat16)
+    part_ref[...] = part.astype(jnp.bfloat16)
+
+
+def join_kernel(part_ref, core_ref, beside_ref, beside_core_ref, joined_ref):
+    width = part_ref.shape[1]
+    own = (part_ref[...].astype(jnp.float32) + core_ref[...].astype(jnp.float32)).astype(jnp.bfloat16)
+    beside = (beside_ref[...].astype(jnp.float32) + beside_core_ref[...].astype(jnp.float32)).astype(jnp.bfloat16)
+    odd = lax.rem(lax.axis_index("row"), 2) == 1
+    joined_ref[:, :width] = jnp.where(odd, beside, own)
+    joined_ref[:, width:] = jnp.where(odd, own, beside)
 
 
 def resid_kernel(own_ref, *refs):
-    got, (stream_ref, scale_ref, scaled_ref, squares_ref, tokens_ref, resid, blocks) = refs[:SQUARE], refs[SQUARE:]
-    unit = own_ref.shape[1]
-    place = lax.rem(lax.axis_index("row"), SQUARE)
-    for step in range(SQUARE):
-        added = got[step][...]
-        if step == 0:
-            added = jnp.where(at_home(), own_ref[...], added)
-        columns = pl.ds(pl.multiple_of((place ^ step) * unit, 128), unit)
+    got, (stream_ref, scale_ref, scaled_ref, squares_ref, tokens_ref, resid, blocks) = refs[:2], refs[2:]
+    width = own_ref.shape[1]
+    for step, added in enumerate(arrange(own_ref, got)):
+        columns = pl.ds(pl.multiple_of((pair_place() ^ step) * width, 128), width)
         resid[:, columns] = stream_ref[:, columns] + added.astype(jnp.float32)
     whole = resid[...]
     scaled_ref[...] = (whole * scale_ref[...][None, :]).astype(jnp.bfloat16)
@@ -276,13 +289,13 @@
         at = slice(start, start + columns)
         lowered = jnp.dot(hidden[...], weight_ref[:, at], preferred_element_type=jnp.float32)
         for block in range(count):
-            blocks_ref[block, :, at] = lowered[rows * block : rows * (block + 1)]
+            blocks_ref[block, :, at] = lowered[rows * block : rows * (block + 1)].astype(jnp.bfloat16)
 
 
 def leave_kernel(tokens_ref, blocks_ref, updated_ref):
     total = tokens_ref[...]
     for block in range(blocks_ref.shape[0]):
-        total = total + blocks_ref[block]
+        total = total + blocks_ref[block].astype(jnp.float32)
     updated_ref[...] = total.astype(jnp.bfloat16)
 
 
@@ -292,7 +305,10 @@
     count = lax.axis_size("row")
     tokens = tok_rows * count
 
-    [pair] = call(pair_kernel, [((2, tok_rows, half), bf16)], hidden_states, from_row(hidden_states, 1))
+    beside = from_row(hidden_states, 1)
+    held = (hidden_states, scale_attn)
+    own, scale_attn = call(bring_kernel, [(v.shape, v.dtype) for v in held], *held)
+    [pair] = call(pair_kernel, [((2, tok_rows, half), bf16)], own, beside)
     pairs = [pair] + [from_row(pair, 2 * step) for step in range(1, count // 2)]
     stream, scaled, squares = call(
         enter_kernel,
@@ -304,22 +320,19 @@
     columns = w_qkv.shape[1]
     part, sent = call(functools.partial(product_kernel, 256), [((tokens, columns), f32), ((tokens, columns), bf16)], scaled, w_qkv)
     unit = columns // 3
-    block = ((tokens, unit), bf16)
-    kept, near, far = call(units_kernel, [block] * 3, part, other_core(sent), squares, squares_other)
+    block, double = ((tokens, unit), bf16), ((tokens, 2 * unit), bf16)
+    near, far = call(units_kernel, [double, block], part, other_core(sent), squares, squares_other)
     [attended] = call(
-        attend_kernel, [block], kept, from_row(near, 1), from_row(far, 2), scratch=[pltpu.VMEM((3, tokens, unit), bf16)]
-    )
-    part, sent = call(
-        out_kernel,
-        [((tokens, unit), f32), block],
-        attended, *spread(attended), w_out,
-        scratch=[pltpu.VMEM((tokens, unit), bf16)],
-    )
-    [attn_out] = call(sum_kernel, [block], part, other_core(sent))
+        attend_kernel, [double], near, from_row(near, 1), from_row(far, 2), from_row(far, 3),
+        scratch=[pltpu.VMEM((3, tokens, 2 * unit), bf16)],
+    )
+    [part] = call(out_kernel, [block], attended, *spread(attended), w_out)
+    across = lax.ppermute(part, ("row", "col"), [(i, i ^ 3) for i in range(2 * count)])
+    [joined] = call(join_kernel, [double], part, other_core(part), from_row(part, 1), across)
     scaled, squares, own = call(
         resid_kernel,
         [((tokens, half), bf16), ((tokens, 128), f32), ((tok_rows, half), f32)],
-        attn_out, *spread(attn_out), stream, scale_mlp,
+        joined, *spread(joined), stream, scale_mlp,
         scratch=[pltpu.VMEM((tokens, half), f32), pltpu.VMEM((count, tok_rows, half), f32)],
     )
     squares_other = other_core(squares)
@@ -331,7 +344,7 @@
     upward, up_sent = call(product, parts, scaled, w_up)
     [lowered] = call(
         functools.partial(down_kernel, 256),
-        [((count, tok_rows, half), f32)],
+        [((count, tok_rows, half), bf16)],
         gate, gate_other, upward, other_core(up_sent), squares, squares_other, w_down,
         scratch=[pltpu.VMEM((tokens, units), bf16)],
     )

time: 72.5 us -> 69.3 us (0.956)
  starting transfers between devices: 30.2 us -> 24.8 us
  waiting for transfers between devices: 16 us -> 19 us
  blocking collectives: 12.2 us -> 10.6 us
  local copies, waits for them, and re-layouts: 1.51 us -> 2.26 us
    ppermute x8 -> x4, starting transfers between devices: 8.4 us -> 3.61 us  [spread(): got.append(lax.ppermute(block, ('row', 'col'), pairs))]
    ppermute x6, starting transfers between devices: 12.5 us -> 8.77 us  [other_core(): return lax.ppermute(block, 'col', [(0, 1), (1, 0)])]
    ppermute x8 -> x4, waiting for transfers between devices: 3.34 us -> 6.14 us  [spread(): got.append(lax.ppermute(block, ('row', 'col'), pairs))]
    ppermute x6 -> x8, starting transfers between devices: 9.39 us -> 11.5 us  [from_row(): return lax.ppermute(block, 'row', [(i, i ^ step) for i in range(count)])]
    all_to_all x1, blocking collectives: 12.2 us -> 10.6 us  [few_rows(): lax.all_to_all(lowered, 'row', split_axis=0, concat_axis=0, tiled=True)]
    ppermute x6 -> x8, waiting for transfers between devices: 9.8 us -> 10.9 us  [from_row(): return lax.ppermute(block, 'row', [(i, i ^ step) for i in range(count)])]
    ppermute x0 -> x1, starting transfers between devices: none -> 0.91 us  [few_rows(): lax.ppermute(part, ('row', 'col'), [(i, i ^ 3) for i in range(2 * count)])]
    ppermute x6, waiting for transfers between devices: 2.83 us -> 1.98 us  [other_core(): return lax.ppermute(block, 'col', [(0, 1), (1, 0)])]
  transfers between devices with their start and end apart: 20 -> 19, of which waited for: 12 -> 9; matrix products, arithmetic and copies ran while one was open for 0% -> 0% of each run, Pallas kernels for 4% -> 4%
where the time goes in v3:
time: 69.3 us; the launch traced here: 68.9 us
  starting transfers between devices  24.8 us (36%)
  waiting for transfers between devices  19 us (27%)
  Pallas kernels  12 us (17%)
  blocking collectives  10.6 us (15%)
  local copies, waits for them, and re-layouts  2.26 us (3%)
    pallas_call x13, Pallas kernels, call(): pl.pallas_call(kernel, out_shape=[jax.ShapeDtypeStruct(*out) for out in o...  12 us
    ppermute x8, starting transfers between devices, from_row(): return lax.ppermute(block, 'row', [(i, i ^ step) for i in range(count)])  11.5 us
    ppermute x8, waiting for transfers between devices, from_row(): return lax.ppermute(block, 'row', [(i, i ^ step) for i in range(count)])  10.9 us
    all_to_all x1, blocking collectives, few_rows(): lax.all_to_all(lowered, 'row', split_axis=0, concat_axis=0, tiled=True)  10.6 us
    ppermute x6, starting transfers between devices, other_core(): return lax.ppermute(block, 'col', [(0, 1), (1, 0)])  8.77 us
    ppermute x4, waiting for transfers between devices, spread(): got.append(lax.ppermute(block, ('row', 'col'), pairs))  6.14 us
    ppermute x4, starting transfers between devices, spread(): got.append(lax.ppermute(block, ('row', 'col'), pairs))  3.61 us
    unnamed x42, local copies, waits for them, and re-layouts  2.26 us
  transfers between devices with their start and end apart: 19, of which 9 were waited for; matrix products, arithmetic and copies ran while one was open for 0% of the time, Pallas kernels for 4%

profile of v3, /device:TPU:0, one launch (start us, length us, event | category | flops | bytes accessed | tf_op | source)
XLA Modules:
  0.0 68.9 jit_solution(14216817006714039027)
XLA Ops:
  0.0 2.9 %collective-permute-start = (bf16[2,3072]{1,0:T(2,128)(2,1)}, bf16[2,3072]{1,0:T(2,128)(2,1)S(1)}, u32[]{:S(2)}, u32[]{:S(2)}) collective-permute-start(bf16[2,3072]{1,0:T(2,128)(2,1)} %refs_0_.1), channel_id=1, source_target_pairs={{0,2},{2,0},{4,6},{6,4},{8,10},{10,8},{12,14},{14,12},{1,3},{3,1},... | collective-permute-start | bytes 36872 | tf_op jit(solution)/shard_map/ppermute | solution.py:132
  2.9 1.5 %copy-done.1 = f32[3072]{0:T(1024)S(1)} copy-done((f32[3072]{0:T(1024)S(1)}, f32[3072]{0:T(1024)}, u32[]{:S(2)}) %copy-start.1) | copy-done | bytes 12312
  5.1 1.8 %collective-permute-start.1 = (bf16[2,2,3072]{2,1,0:T(2,128)(2,1)S(1)}, bf16[2,2,3072]{2,1,0:T(2,128)(2,1)S(1)}, u32[]{:S(2)}, u32[]{:S(2)}) collective-permute-start(bf16[2,2,3072]{2,1,0:T(2,128)(2,1)S(1)} %shard_map.83.refs_0_), channel_id=1, source_target_pairs={{0,4},{2,6},{4,0},{6,2},{8,12},{10,14},{12,8},{14,10},{1,5},{3,7},... | collective-permute-start | bytes 73736 | tf_op jit(solution)/shard_map/ppermute | solution.py:132
  6.9 2.6 %collective-permute-start.2 = (bf16[2,2,3072]{2,1,0:T(2,128)(2,1)S(1)}, bf16[2,2,3072]{2,1,0:T(2,128)(2,1)S(1)}, u32[]{:S(2)}, u32[]{:S(2)}) collective-permute-start(bf16[2,2,3072]{2,1,0:T(2,128)(2,1)S(1)} %shard_map.83.refs_0_), channel_id=1, source_target_pairs={{0,8},{2,10},{4,12},{6,14},{8,0},{10,2},{12,4},{14,6},{1,9},{3,11}... | collective-permute-start | bytes 73736 | tf_op jit(solution)/shard_map/ppermute | solution.py:132
  9.6 2.1 %collective-permute-done.2.refs_2_ = bf16[2,2,3072]{2,1,0:T(2,128)(2,1)S(1)} collective-permute-done((bf16[2,2,3072]{2,1,0:T(2,128)(2,1)S(1)}, bf16[2,2,3072]{2,1,0:T(2,128)(2,1)S(1)}, u32[]{:S(2)}, u32[]{:S(2)}) %collective-permute-start.2) | collective-permute-done | bytes 24608 | tf_op jit(solution)/shard_map/ppermute | solution.py:132
  11.7 3.4 %collective-permute-done.3.refs_3_ = bf16[2,2,3072]{2,1,0:T(2,128)(2,1)S(1)} collective-permute-done((bf16[2,2,3072]{2,1,0:T(2,128)(2,1)S(1)}, bf16[2,2,3072]{2,1,0:T(2,128)(2,1)S(1)}, u32[]{:S(2)}, u32[]{:S(2)}) %collective-permute-start.3) | collective-permute-done | bytes 24608 | tf_op jit(solution)/shard_map/ppermute | solution.py:132
  15.4 1.9 %shard_map.85 = (f32[16,2304]{1,0:T(8,128)S(1)}, bf16[16,2304]{1,0:T(8,128)(2,1)S(1)}) custom-call(bf16[16,3072]{1,0:T(8,128)(2,1)S(1)} %get-tuple-element.23.left_ref, bf16[3072,2304]{1,0:T(8,128)(2,1)S(1)} %copy-done), custom_call_target="tpu_custom_call" | custom-call | flops 2000000000 | bytes 100000 | tf_op jit(solution)/shard_map/pallas_call | solution.py:115
  18.8 1.6 %collective-permute-start.6 = (bf16[16,1536]{1,0:T(8,128)(2,1)S(1)}, bf16[16,1536]{1,0:T(8,128)(2,1)S(1)}, u32[]{:S(2)}, u32[]{:S(2)}) collective-permute-start(bf16[16,1536]{1,0:T(8,128)(2,1)S(1)} %get-tuple-element.27.kept_ref), channel_id=1, source_target_pairs={{0,2},{2,0},{4,6},{6,4},{8,10},{10,8},{12,14},{14,12},{1,3},{3,1},... | collective-permute-start | bytes 147464 | tf_op jit(solution)/shard_map/ppermute | solution.py:132
  20.3 2.0 %collective-permute-start.8 = (bf16[16,768]{1,0:T(8,128)(2,1)S(1)}, bf16[16,768]{1,0:T(8,128)(2,1)S(1)}, u32[]{:S(2)}, u32[]{:S(2)}) collective-permute-start(bf16[16,768]{1,0:T(8,128)(2,1)S(1)} %get-tuple-element.28), channel_id=1, source_target_pairs={{0,6},{2,4},{4,2},{6,0},{8,14},{10,12},{12,10},{14,8},{1,7},{3,5},... | collective-permute-start | bytes 73736 | tf_op jit(solution)/shard_map/ppermute | solution.py:132
  22.3 1.8 %collective-permute-done.7.straight_ref = bf16[16,768]{1,0:T(8,128)(2,1)S(1)} collective-permute-done((bf16[16,768]{1,0:T(8,128)(2,1)S(1)}, bf16[16,768]{1,0:T(8,128)(2,1)S(1)}, u32[]{:S(2)}, u32[]{:S(2)}) %collective-permute-start.7) | collective-permute-done | bytes 24608 | tf_op jit(solution)/shard_map/ppermute | solution.py:132
  24.1 0.9 %collective-permute-done.8.across_ref = bf16[16,768]{1,0:T(8,128)(2,1)S(1)} collective-permute-done((bf16[16,768]{1,0:T(8,128)(2,1)S(1)}, bf16[16,768]{1,0:T(8,128)(2,1)S(1)}, u32[]{:S(2)}, u32[]{:S(2)}) %collective-permute-start.8) | collective-permute-done | bytes 24608 | tf_op jit(solution)/shard_map/ppermute | solution.py:132
  26.5 2.1 %collective-permute-start.10 = (bf16[16,1536]{1,0:T(8,128)(2,1)S(1)}, bf16[16,1536]{1,0:T(8,128)(2,1)S(1)}, u32[]{:S(2)}, u32[]{:S(2)}) collective-permute-start(bf16[16,1536]{1,0:T(8,128)(2,1)S(1)} %shard_map.87.own_ref), channel_id=1, source_target_pairs={{0,4},{1,12},{2,6},{3,14},{4,0},{5,8},{6,2},{7,10},{9,13},{8,5},{1... | collective-permute-start | bytes 147464 | tf_op jit(solution)/shard_map/ppermute | solution.py:144
  28.6 2.1 %collective-permute-done.10.refs_1_ = bf16[16,1536]{1,0:T(8,128)(2,1)S(1)} collective-permute-done((bf16[16,1536]{1,0:T(8,128)(2,1)S(1)}, bf16[16,1536]{1,0:T(8,128)(2,1)S(1)}, u32[]{:S(2)}, u32[]{:S(2)}) %collective-permute-start.10) | collective-permute-done | bytes 49184 | tf_op jit(solution)/shard_map/ppermute | solution.py:144
  31.4 3.6 %collective-permute-start.11 = (bf16[16,768]{1,0:T(8,128)(2,1)S(1)}, bf16[16,768]{1,0:T(8,128)(2,1)S(1)}, u32[]{:S(2)}, u32[]{:S(2)}) collective-permute-start(bf16[16,768]{1,0:T(8,128)(2,1)S(1)} %shard_map.88.part_ref), channel_id=1, source_target_pairs={{0,1},{1,0},{2,3},{3,2},{4,5},{5,4},{6,7},{7,6},{8,9},{9,8},{10,11... | collective-permute-start | bytes 73736 | tf_op jit(solution)/shard_map/ppermute | solution.py:127
  35.5 0.9 %collective-permute-start.13 = (bf16[16,768]{1,0:T(8,128)(2,1)S(1)}, bf16[16,768]{1,0:T(8,128)(2,1)S(1)}, u32[]{:S(2)}, u32[]{:S(2)}) collective-permute-start(bf16[16,768]{1,0:T(8,128)(2,1)S(1)} %shard_map.88.part_ref), channel_id=1, source_target_pairs={{0,3},{1,2},{2,1},{3,0},{4,7},{5,6},{6,5},{7,4},{8,11},{9,10},{10,... | collective-permute-start | bytes 73736 | tf_op jit(solution)/shard_map/ppermute | solution.py:330
  36.4 2.6 %collective-permute-done.12.beside_ref = bf16[16,768]{1,0:T(8,128)(2,1)S(1)} collective-permute-done((bf16[16,768]{1,0:T(8,128)(2,1)S(1)}, bf16[16,768]{1,0:T(8,128)(2,1)S(1)}, u32[]{:S(2)}, u32[]{:S(2)}) %collective-permute-start.12) | collective-permute-done | bytes 24608 | tf_op jit(solution)/shard_map/ppermute | solution.py:132
  39.8 4.1 %collective-permute-done.15.refs_1_ = bf16[16,1536]{1,0:T(8,128)(2,1)S(1)} collective-permute-done((bf16[16,1536]{1,0:T(8,128)(2,1)S(1)}, bf16[16,1536]{1,0:T(8,128)(2,1)S(1)}, u32[]{:S(2)}, u32[]{:S(2)}) %collective-permute-start.15) | collective-permute-done | bytes 49184 | tf_op jit(solution)/shard_map/ppermute | solution.py:144
  44.1 2.5 %shard_map.91 = (f32[16,3072]{1,0:T(8,128)S(1)}, bf16[16,3072]{1,0:T(8,128)(2,1)S(1)}) custom-call(bf16[16,3072]{1,0:T(8,128)(2,1)S(1)} %get-tuple-element.31.left_ref, bf16[3072,3072]{1,0:T(8,128)(2,1)S(1)} %bitcast.1), custom_call_target="tpu_custom_call" | custom-call | flops 2000000000 | bytes 100000 | tf_op jit(solution)/shard_map/pallas_call | solution.py:115
  46.7 2.7 %collective-permute-start.16 = (bf16[16,3072]{1,0:T(8,128)(2,1)S(1)}, bf16[16,3072]{1,0:T(8,128)(2,1)S(1)}, u32[]{:S(2)}, u32[]{:S(2)}) collective-permute-start(bf16[16,3072]{1,0:T(8,128)(2,1)S(1)} %get-tuple-element.33), channel_id=1, source_target_pairs={{0,1},{1,0},{2,3},{3,2},{4,5},{5,4},{6,7},{7,6},{8,9},{9,8},{10,11... | collective-permute-start | bytes 294920 | tf_op jit(solution)/shard_map/ppermute | solution.py:127
  49.4 2.5 %shard_map.92 = (f32[16,3072]{1,0:T(8,128)S(1)}, bf16[16,3072]{1,0:T(8,128)(2,1)S(1)}) custom-call(bf16[16,3072]{1,0:T(8,128)(2,1)S(1)} %get-tuple-element.31.left_ref, bf16[3072,3072]{1,0:T(8,128)(2,1)S(1)} %bitcast.3), custom_call_target="tpu_custom_call" | custom-call | flops 2000000000 | bytes 100000 | tf_op jit(solution)/shard_map/pallas_call | solution.py:115
  52.0 1.9 %collective-permute-start.17 = (bf16[16,3072]{1,0:T(8,128)(2,1)S(1)}, bf16[16,3072]{1,0:T(8,128)(2,1)S(1)}, u32[]{:S(2)}, u32[]{:S(2)}) collective-permute-start(bf16[16,3072]{1,0:T(8,128)(2,1)S(1)} %get-tuple-element.35), channel_id=1, source_target_pairs={{0,1},{1,0},{2,3},{3,2},{4,5},{5,4},{6,7},{7,6},{8,9},{9,8},{10,11... | collective-permute-start | bytes 294920 | tf_op jit(solution)/shard_map/ppermute | solution.py:127
  53.9 1.1 %collective-permute-done.18.refs_5_ = f32[16,128]{1,0:T(8,128)S(1)} collective-permute-done((f32[16,128]{1,0:T(8,128)S(1)}, f32[16,128]{1,0:T(8,128)S(1)}, u32[]{:S(2)}, u32[]{:S(2)}) %collective-permute-start.18) | collective-permute-done | bytes 8224 | tf_op jit(solution)/shard_map/ppermute | solution.py:127
  55.1 2.6 %shard_map.93 = bf16[8,2,3072]{2,1,0:T(2,128)(2,1)S(1)} custom-call(f32[16,3072]{1,0:T(8,128)S(1)} %get-tuple-element.32.refs_0_, bf16[16,3072]{1,0:T(8,128)(2,1)S(1)} %collective-permute-done.16.refs_1_, f32[16,3072]{1,0:T(8,128)S(1)} %get-tuple-element.34.refs_2_, bf16[16,3072]{1,0:T(8,128)(2,1)S(1)} %collective-permute-done.17.refs_3_, ...), custom_call_target="tpu_custom_call" | custom-call | flops 2000000000 | bytes 100000 | tf_op jit(solution)/shard_map/pallas_call | solution.py:115
  57.7 10.6 %all_to_all.5.blocks_ref = bf16[8,2,3072]{2,1,0:T(2,128)(2,1)S(1)} all-to-all(bf16[8,2,3072]{2,1,0:T(2,128)(2,1)S(1)} %shard_map.93), channel_id=1, replica_groups=mesh['groups'=2,'row'=8,'col'=2] {'row'}, dimensions={0} | all-to-all | bytes 196608 | tf_op jit(solution)/shard_map/all_to_all | solution.py:351
  (74 shorter events, 6.7 us)
Async XLA Ops:
  0.0 5.1 %collective-permute-start = (bf16[2,3072]{1,0:T(2,128)(2,1)}, bf16[2,3072]{1,0:T(2,128)(2,1)S(1)}, u32[]{:S(2)}, u32[]{:S(2)}) collective-permute-start(bf16[2,3072]{1,0:T(2,128)(2,1)} %refs_0_.1), channel_id=1, source_target_pairs={{0,2},{2,0},{4,6},{6,4},{8,10},{10,8},{12,14},{14,12},{1,3},{3,1},... | collective-permute-start | bytes 36872 | tf_op jit(solution)/shard_map/ppermute | solution.py:132
  5.1 25.5 %slice-start.15 = ((s8[4718592]{0:T(1024)(128)(4,1)}), s8[4194304]{0:T(1024)(128)(4,1)S(1)}, s32[]{:S(2)}) async-start(s8[4718592]{0:T(1024)(128)(4,1)} %bitcast.6), calls=%async_computation.16 | async-start | bytes 8388608
  5.1 4.5 %collective-permute-start.1 = (bf16[2,2,3072]{2,1,0:T(2,128)(2,1)S(1)}, bf16[2,2,3072]{2,1,0:T(2,128)(2,1)S(1)}, u32[]{:S(2)}, u32[]{:S(2)}) collective-permute-start(bf16[2,2,3072]{2,1,0:T(2,128)(2,1)S(1)} %shard_map.83.refs_0_), channel_id=1, source_target_pairs={{0,4},{2,6},{4,0},{6,2},{8,12},{10,14},{12,8},{14,10},{1,5},{3,7},... | collective-permute-start | bytes 73736 | tf_op jit(solution)/shard_map/ppermute | solution.py:132
  6.9 4.8 %collective-permute-start.2 = (bf16[2,2,3072]{2,1,0:T(2,128)(2,1)S(1)}, bf16[2,2,3072]{2,1,0:T(2,128)(2,1)S(1)}, u32[]{:S(2)}, u32[]{:S(2)}) collective-permute-start(bf16[2,2,3072]{2,1,0:T(2,128)(2,1)S(1)} %shard_map.83.refs_0_), channel_id=1, source_target_pairs={{0,8},{2,10},{4,12},{6,14},{8,0},{10,2},{12,4},{14,6},{1,9},{3,11}... | collective-permute-start | bytes 73736 | tf_op jit(solution)/shard_map/ppermute | solution.py:132
  9.5 5.6 %collective-permute-start.3 = (bf16[2,2,3072]{2,1,0:T(2,128)(2,1)S(1)}, bf16[2,2,3072]{2,1,0:T(2,128)(2,1)S(1)}, u32[]{:S(2)}, u32[]{:S(2)}) collective-permute-start(bf16[2,2,3072]{2,1,0:T(2,128)(2,1)S(1)} %shard_map.83.refs_0_), channel_id=1, source_target_pairs={{0,12},{2,14},{4,8},{6,10},{8,4},{10,6},{12,0},{14,2},{1,13},{3,15... | collective-permute-start | bytes 73736 | tf_op jit(solution)/shard_map/ppermute | solution.py:132
  15.3 28.6 %copy-start.3 = (f32[3072]{0:T(1024)S(1)}, f32[3072]{0:T(1024)}, u32[]{:S(2)}) copy-start(f32[3072]{0:T(1024)} %refs_3_.1) | copy-start | bytes 36868
  15.4 28.7 %slice-start = ((s8[18874368]{0:T(1024)(128)(4,1)}), s8[4194304]{0:T(1024)(128)(4,1)S(1)}, s32[]{:S(2)}) async-start(s8[18874368]{0:T(1024)(128)(4,1)} %bitcast), calls=%async_computation.1 | async-start | bytes 8388608
  15.4 28.7 %slice-start.1 = ((s8[18874368]{0:T(1024)(128)(4,1)}), s8[4194304]{0:T(1024)(128)(4,1)S(1)}, s32[]{:S(2)}) async-start(s8[18874368]{0:T(1024)(128)(4,1)} %bitcast), calls=%async_computation.2 | async-start | bytes 8388608
  17.3 1.4 %collective-permute-start.4 = (bf16[16,2304]{1,0:T(8,128)(2,1)S(1)}, bf16[16,2304]{1,0:T(8,128)(2,1)S(1)}, u32[]{:S(2)}, u32[]{:S(2)}) collective-permute-start(bf16[16,2304]{1,0:T(8,128)(2,1)S(1)} %get-tuple-element.25), channel_id=1, source_target_pairs={{0,1},{1,0},{2,3},{3,2},{4,5},{5,4},{6,7},{7,6},{8,9},{9,8},{10,11... | collective-permute-start | bytes 221192 | tf_op jit(solution)/shard_map/ppermute | solution.py:127
  17.3 1.3 %collective-permute-start.5 = (f32[16,128]{1,0:T(8,128)S(1)}, f32[16,128]{1,0:T(8,128)S(1)}, u32[]{:S(2)}, u32[]{:S(2)}) collective-permute-start(f32[16,128]{1,0:T(8,128)S(1)} %get-tuple-element.26.squares_ref), channel_id=1, source_target_pairs={{0,1},{1,0},{2,3},{3,2},{4,5},{5,4},{6,7},{7,6},{8,9},{9,8},{10,11... | collective-permute-start | bytes 24584 | tf_op jit(solution)/shard_map/ppermute | solution.py:127
  18.7 25.4 %slice-start.2 = ((s8[18874368]{0:T(1024)(128)(4,1)}), s8[4194304]{0:T(1024)(128)(4,1)S(1)}, s32[]{:S(2)}) async-start(s8[18874368]{0:T(1024)(128)(4,1)} %bitcast), calls=%async_computation.3 | async-start | bytes 8388608
  18.8 6.3 %collective-permute-start.6 = (bf16[16,1536]{1,0:T(8,128)(2,1)S(1)}, bf16[16,1536]{1,0:T(8,128)(2,1)S(1)}, u32[]{:S(2)}, u32[]{:S(2)}) collective-permute-start(bf16[16,1536]{1,0:T(8,128)(2,1)S(1)} %get-tuple-element.27.kept_ref), channel_id=1, source_target_pairs={{0,2},{2,0},{4,6},{6,4},{8,10},{10,8},{12,14},{14,12},{1,3},{3,1},... | collective-permute-start | bytes 147464 | tf_op jit(solution)/shard_map/ppermute | solution.py:132
  20.3 3.8 %collective-permute-start.7 = (bf16[16,768]{1,0:T(8,128)(2,1)S(1)}, bf16[16,768]{1,0:T(8,128)(2,1)S(1)}, u32[]{:S(2)}, u32[]{:S(2)}) collective-permute-start(bf16[16,768]{1,0:T(8,128)(2,1)S(1)} %get-tuple-element.28), channel_id=1, source_target_pairs={{0,4},{2,6},{4,0},{6,2},{8,12},{10,14},{12,8},{14,10},{1,5},{3,7},... | collective-permute-start | bytes 73736 | tf_op jit(solution)/shard_map/ppermute | solution.py:132
  20.3 4.7 %collective-permute-start.8 = (bf16[16,768]{1,0:T(8,128)(2,1)S(1)}, bf16[16,768]{1,0:T(8,128)(2,1)S(1)}, u32[]{:S(2)}, u32[]{:S(2)}) collective-permute-start(bf16[16,768]{1,0:T(8,128)(2,1)S(1)} %get-tuple-element.28), channel_id=1, source_target_pairs={{0,6},{2,4},{4,2},{6,0},{8,14},{10,12},{12,10},{14,8},{1,7},{3,5},... | collective-permute-start | bytes 73736 | tf_op jit(solution)/shard_map/ppermute | solution.py:132
  25.7 2.9 %collective-permute-start.9 = (bf16[16,1536]{1,0:T(8,128)(2,1)S(1)}, bf16[16,1536]{1,0:T(8,128)(2,1)S(1)}, u32[]{:S(2)}, u32[]{:S(2)}) collective-permute-start(bf16[16,1536]{1,0:T(8,128)(2,1)S(1)} %shard_map.87.own_ref), channel_id=1, source_target_pairs={{1,8},{3,10},{5,12},{7,14},{8,1},{10,3},{12,5},{14,7},{17,24},{19,... | collective-permute-start | bytes 147464 | tf_op jit(solution)/shard_map/ppermute | solution.py:144
  26.5 4.2 %collective-permute-start.10 = (bf16[16,1536]{1,0:T(8,128)(2,1)S(1)}, bf16[16,1536]{1,0:T(8,128)(2,1)S(1)}, u32[]{:S(2)}, u32[]{:S(2)}) collective-permute-start(bf16[16,1536]{1,0:T(8,128)(2,1)S(1)} %shard_map.87.own_ref), channel_id=1, source_target_pairs={{0,4},{1,12},{2,6},{3,14},{4,0},{5,8},{6,2},{7,10},{9,13},{8,5},{1... | collective-permute-start | bytes 147464 | tf_op jit(solution)/shard_map/ppermute | solution.py:144
  31.4 5.0 %collective-permute-start.11 = (bf16[16,768]{1,0:T(8,128)(2,1)S(1)}, bf16[16,768]{1,0:T(8,128)(2,1)S(1)}, u32[]{:S(2)}, u32[]{:S(2)}) collective-permute-start(bf16[16,768]{1,0:T(8,128)(2,1)S(1)} %shard_map.88.part_ref), channel_id=1, source_target_pairs={{0,1},{1,0},{2,3},{3,2},{4,5},{5,4},{6,7},{7,6},{8,9},{9,8},{10,11... | collective-permute-start | bytes 73736 | tf_op jit(solution)/shard_map/ppermute | solution.py:127
  35.0 4.0 %collective-permute-start.12 = (bf16[16,768]{1,0:T(8,128)(2,1)S(1)}, bf16[16,768]{1,0:T(8,128)(2,1)S(1)}, u32[]{:S(2)}, u32[]{:S(2)}) collective-permute-start(bf16[16,768]{1,0:T(8,128)(2,1)S(1)} %shard_map.88.part_ref), channel_id=1, source_target_pairs={{0,2},{2,0},{4,6},{6,4},{8,10},{10,8},{12,14},{14,12},{1,3},{3,1},... | collective-permute-start | bytes 73736 | tf_op jit(solution)/shard_map/ppermute | solution.py:132
  35.5 3.5 %collective-permute-start.13 = (bf16[16,768]{1,0:T(8,128)(2,1)S(1)}, bf16[16,768]{1,0:T(8,128)(2,1)S(1)}, u32[]{:S(2)}, u32[]{:S(2)}) collective-permute-start(bf16[16,768]{1,0:T(8,128)(2,1)S(1)} %shard_map.88.part_ref), channel_id=1, source_target_pairs={{0,3},{1,2},{2,1},{3,0},{4,7},{5,6},{6,5},{7,4},{8,11},{9,10},{10,... | collective-permute-start | bytes 73736 | tf_op jit(solution)/shard_map/ppermute | solution.py:330
  39.1 0.8 %collective-permute-start.14 = (bf16[16,1536]{1,0:T(8,128)(2,1)S(1)}, bf16[16,1536]{1,0:T(8,128)(2,1)S(1)}, u32[]{:S(2)}, u32[]{:S(2)}) collective-permute-start(bf16[16,1536]{1,0:T(8,128)(2,1)S(1)} %shard_map.89.own_ref), channel_id=1, source_target_pairs={{1,8},{3,10},{5,12},{7,14},{8,1},{10,3},{12,5},{14,7},{17,24},{19,... | collective-permute-start | bytes 147464 | tf_op jit(solution)/shard_map/ppermute | solution.py:144
  39.7 4.2 %collective-permute-start.15 = (bf16[16,1536]{1,0:T(8,128)(2,1)S(1)}, bf16[16,1536]{1,0:T(8,128)(2,1)S(1)}, u32[]{:S(2)}, u32[]{:S(2)}) collective-permute-start(bf16[16,1536]{1,0:T(8,128)(2,1)S(1)} %shard_map.89.own_ref), channel_id=1, source_target_pairs={{0,4},{1,12},{2,6},{3,14},{4,0},{5,8},{6,2},{7,10},{9,13},{8,5},{1... | collective-permute-start | bytes 147464 | tf_op jit(solution)/shard_map/ppermute | solution.py:144
  46.7 8.4 %collective-permute-start.16 = (bf16[16,3072]{1,0:T(8,128)(2,1)S(1)}, bf16[16,3072]{1,0:T(8,128)(2,1)S(1)}, u32[]{:S(2)}, u32[]{:S(2)}) collective-permute-start(bf16[16,3072]{1,0:T(8,128)(2,1)S(1)} %get-tuple-element.33), channel_id=1, source_target_pairs={{0,1},{1,0},{2,3},{3,2},{4,5},{5,4},{6,7},{7,6},{8,9},{9,8},{10,11... | collective-permute-start | bytes 294920 | tf_op jit(solution)/shard_map/ppermute | solution.py:127
  52.0 3.1 %collective-permute-start.17 = (bf16[16,3072]{1,0:T(8,128)(2,1)S(1)}, bf16[16,3072]{1,0:T(8,128)(2,1)S(1)}, u32[]{:S(2)}, u32[]{:S(2)}) collective-permute-start(bf16[16,3072]{1,0:T(8,128)(2,1)S(1)} %get-tuple-element.35), channel_id=1, source_target_pairs={{0,1},{1,0},{2,3},{3,2},{4,5},{5,4},{6,7},{7,6},{8,9},{9,8},{10,11... | collective-permute-start | bytes 294920 | tf_op jit(solution)/shard_map/ppermute | solution.py:127
  53.9 1.2 %collective-permute-start.18 = (f32[16,128]{1,0:T(8,128)S(1)}, f32[16,128]{1,0:T(8,128)S(1)}, u32[]{:S(2)}, u32[]{:S(2)}) collective-permute-start(f32[16,128]{1,0:T(8,128)S(1)} %get-tuple-element.36.refs_4_), channel_id=1, source_target_pairs={{0,1},{1,0},{2,3},{3,2},{4,5},{5,4},{6,7},{7,6},{8,9},{9,8},{10,11... | collective-permute-start | bytes 24584 | tf_op jit(solution)/shard_map/ppermute | solution.py:127
  (16 other events, 200.1 us)

commit v4 on v3

--- a/solution.py
+++ b/solution.py
@@ -328,11 +328,12 @@
     )
     [part] = call(out_kernel, [block], attended, *spread(attended), w_out)
     across = lax.ppermute(part, ("row", "col"), [(i, i ^ 3) for i in range(2 * count)])
-    [joined] = call(join_kernel, [double], part, other_core(part), from_row(part, 1), across)
+    [joined] = call(join_kernel, [double], part, other_core(part), from_row(part, 1), across, flops=10 * 10**8)
     scaled, squares, own = call(
         resid_kernel,
         [((tokens, half), bf16), ((tokens, 128), f32), ((tok_rows, half), f32)],
         joined, *spread(joined), stream, scale_mlp,
+        flops=5 * 10**8,
         scratch=[pltpu.VMEM((tokens, half), f32), pltpu.VMEM((count, tok_rows, half), f32)],
     )
     squares_other = other_core(squares)

time: 69.3 us -> 68.2 us (0.984)
  starting transfers between devices: 24.8 us -> 23.6 us
    ppermute x6, starting transfers between devices: 8.77 us -> 7.67 us  [other_core(): return lax.ppermute(block, 'col', [(0, 1), (1, 0)])]
where the time goes in v4:
time: 68.2 us; the launch traced here: 67.8 us
  starting transfers between devices  23.6 us (35%)
  waiting for transfers between devices  19.1 us (28%)
  Pallas kernels  12 us (18%)
  blocking collectives  10.6 us (16%)
  local copies, waits for them, and re-layouts  2.26 us (3%)
    pallas_call x13, Pallas kernels, call(): pl.pallas_call(kernel, out_shape=[jax.ShapeDtypeStruct(*out) for out in o...  12 us
    ppermute x8, starting transfers between devices, from_row(): return lax.ppermute(block, 'row', [(i, i ^ step) for i in range(count)])  11.5 us
    ppermute x8, waiting for transfers between devices, from_row(): return lax.ppermute(block, 'row', [(i, i ^ step) for i in range(count)])  10.9 us
    all_to_all x1, blocking collectives, few_rows(): lax.all_to_all(lowered, 'row', split_axis=0, concat_axis=0, tiled=True)  10.6 us
    ppermute x6, starting transfers between devices, other_core(): return lax.ppermute(block, 'col', [(0, 1), (1, 0)])  7.67 us
    ppermute x4, waiting for transfers between devices, spread(): got.append(lax.ppermute(block, ('row', 'col'), pairs))  6.14 us
    ppermute x4, starting transfers between devices, spread(): got.append(lax.ppermute(block, ('row', 'col'), pairs))  3.61 us
    unnamed x42, local copies, waits for them, and re-layouts  2.26 us
  transfers between devices with their start and end apart: 19, of which 9 were waited for; matrix products, arithmetic and copies ran while one was open for 0% of the time, Pallas kernels for 4%

profile of v4, /device:TPU:0, one launch (start us, length us, event | category | flops | bytes accessed | tf_op | source)
XLA Modules:
  0.0 67.8 jit_solution(4248123993606339922)
XLA Ops:
  0.0 2.9 %collective-permute-start = (bf16[2,3072]{1,0:T(2,128)(2,1)}, bf16[2,3072]{1,0:T(2,128)(2,1)S(1)}, u32[]{:S(2)}, u32[]{:S(2)}) collective-permute-start(bf16[2,3072]{1,0:T(2,128)(2,1)} %refs_0_.1), channel_id=1, source_target_pairs={{0,2},{2,0},{4,6},{6,4},{8,10},{10,8},{12,14},{14,12},{1,3},{3,1},... | collective-permute-start | bytes 36872 | tf_op jit(solution)/shard_map/ppermute | solution.py:132
  2.9 1.5 %copy-done.1 = f32[3072]{0:T(1024)S(1)} copy-done((f32[3072]{0:T(1024)S(1)}, f32[3072]{0:T(1024)}, u32[]{:S(2)}) %copy-start.1) | copy-done | bytes 12312
  5.1 1.8 %collective-permute-start.1 = (bf16[2,2,3072]{2,1,0:T(2,128)(2,1)S(1)}, bf16[2,2,3072]{2,1,0:T(2,128)(2,1)S(1)}, u32[]{:S(2)}, u32[]{:S(2)}) collective-permute-start(bf16[2,2,3072]{2,1,0:T(2,128)(2,1)S(1)} %shard_map.83.refs_0_), channel_id=1, source_target_pairs={{0,4},{2,6},{4,0},{6,2},{8,12},{10,14},{12,8},{14,10},{1,5},{3,7},... | collective-permute-start | bytes 73736 | tf_op jit(solution)/shard_map/ppermute | solution.py:132
  6.9 2.6 %collective-permute-start.2 = (bf16[2,2,3072]{2,1,0:T(2,128)(2,1)S(1)}, bf16[2,2,3072]{2,1,0:T(2,128)(2,1)S(1)}, u32[]{:S(2)}, u32[]{:S(2)}) collective-permute-start(bf16[2,2,3072]{2,1,0:T(2,128)(2,1)S(1)} %shard_map.83.refs_0_), channel_id=1, source_target_pairs={{0,8},{2,10},{4,12},{6,14},{8,0},{10,2},{12,4},{14,6},{1,9},{3,11}... | collective-permute-start | bytes 73736 | tf_op jit(solution)/shard_map/ppermute | solution.py:132
  9.6 2.1 %collective-permute-done.2.refs_2_ = bf16[2,2,3072]{2,1,0:T(2,128)(2,1)S(1)} collective-permute-done((bf16[2,2,3072]{2,1,0:T(2,128)(2,1)S(1)}, bf16[2,2,3072]{2,1,0:T(2,128)(2,1)S(1)}, u32[]{:S(2)}, u32[]{:S(2)}) %collective-permute-start.2) | collective-permute-done | bytes 24608 | tf_op jit(solution)/shard_map/ppermute | solution.py:132
  11.7 3.4 %collective-permute-done.3.refs_3_ = bf16[2,2,3072]{2,1,0:T(2,128)(2,1)S(1)} collective-permute-done((bf16[2,2,3072]{2,1,0:T(2,128)(2,1)S(1)}, bf16[2,2,3072]{2,1,0:T(2,128)(2,1)S(1)}, u32[]{:S(2)}, u32[]{:S(2)}) %collective-permute-start.3) | collective-permute-done | bytes 24608 | tf_op jit(solution)/shard_map/ppermute | solution.py:132
  15.4 1.9 %shard_map.85 = (f32[16,2304]{1,0:T(8,128)S(1)}, bf16[16,2304]{1,0:T(8,128)(2,1)S(1)}) custom-call(bf16[16,3072]{1,0:T(8,128)(2,1)S(1)} %get-tuple-element.23.left_ref, bf16[3072,2304]{1,0:T(8,128)(2,1)S(1)} %copy-done), custom_call_target="tpu_custom_call" | custom-call | flops 2000000000 | bytes 100000 | tf_op jit(solution)/shard_map/pallas_call | solution.py:115
  18.8 1.6 %collective-permute-start.6 = (bf16[16,1536]{1,0:T(8,128)(2,1)S(1)}, bf16[16,1536]{1,0:T(8,128)(2,1)S(1)}, u32[]{:S(2)}, u32[]{:S(2)}) collective-permute-start(bf16[16,1536]{1,0:T(8,128)(2,1)S(1)} %get-tuple-element.27.kept_ref), channel_id=1, source_target_pairs={{0,2},{2,0},{4,6},{6,4},{8,10},{10,8},{12,14},{14,12},{1,3},{3,1},... | collective-permute-start | bytes 147464 | tf_op jit(solution)/shard_map/ppermute | solution.py:132
  20.3 2.0 %collective-permute-start.8 = (bf16[16,768]{1,0:T(8,128)(2,1)S(1)}, bf16[16,768]{1,0:T(8,128)(2,1)S(1)}, u32[]{:S(2)}, u32[]{:S(2)}) collective-permute-start(bf16[16,768]{1,0:T(8,128)(2,1)S(1)} %get-tuple-element.28), channel_id=1, source_target_pairs={{0,6},{2,4},{4,2},{6,0},{8,14},{10,12},{12,10},{14,8},{1,7},{3,5},... | collective-permute-start | bytes 73736 | tf_op jit(solution)/shard_map/ppermute | solution.py:132
  22.3 1.8 %collective-permute-done.7.straight_ref = bf16[16,768]{1,0:T(8,128)(2,1)S(1)} collective-permute-done((bf16[16,768]{1,0:T(8,128)(2,1)S(1)}, bf16[16,768]{1,0:T(8,128)(2,1)S(1)}, u32[]{:S(2)}, u32[]{:S(2)}) %collective-permute-start.7) | collective-permute-done | bytes 24608 | tf_op jit(solution)/shard_map/ppermute | solution.py:132
  24.2 0.9 %collective-permute-done.8.across_ref = bf16[16,768]{1,0:T(8,128)(2,1)S(1)} collective-permute-done((bf16[16,768]{1,0:T(8,128)(2,1)S(1)}, bf16[16,768]{1,0:T(8,128)(2,1)S(1)}, u32[]{:S(2)}, u32[]{:S(2)}) %collective-permute-start.8) | collective-permute-done | bytes 24608 | tf_op jit(solution)/shard_map/ppermute | solution.py:132
  26.5 2.1 %collective-permute-start.10 = (bf16[16,1536]{1,0:T(8,128)(2,1)S(1)}, bf16[16,1536]{1,0:T(8,128)(2,1)S(1)}, u32[]{:S(2)}, u32[]{:S(2)}) collective-permute-start(bf16[16,1536]{1,0:T(8,128)(2,1)S(1)} %shard_map.87.own_ref), channel_id=1, source_target_pairs={{0,4},{1,12},{2,6},{3,14},{4,0},{5,8},{6,2},{7,10},{9,13},{8,5},{1... | collective-permute-start | bytes 147464 | tf_op jit(solution)/shard_map/ppermute | solution.py:144
  28.6 2.1 %collective-permute-done.10.refs_1_ = bf16[16,1536]{1,0:T(8,128)(2,1)S(1)} collective-permute-done((bf16[16,1536]{1,0:T(8,128)(2,1)S(1)}, bf16[16,1536]{1,0:T(8,128)(2,1)S(1)}, u32[]{:S(2)}, u32[]{:S(2)}) %collective-permute-start.10) | collective-permute-done | bytes 49184 | tf_op jit(solution)/shard_map/ppermute | solution.py:144
  31.4 3.6 %collective-permute-start.11 = (bf16[16,768]{1,0:T(8,128)(2,1)S(1)}, bf16[16,768]{1,0:T(8,128)(2,1)S(1)}, u32[]{:S(2)}, u32[]{:S(2)}) collective-permute-start(bf16[16,768]{1,0:T(8,128)(2,1)S(1)} %shard_map.88.part_ref), channel_id=1, source_target_pairs={{0,1},{1,0},{2,3},{3,2},{4,5},{5,4},{6,7},{7,6},{8,9},{9,8},{10,11... | collective-permute-start | bytes 73736 | tf_op jit(solution)/shard_map/ppermute | solution.py:127
  35.5 0.9 %collective-permute-start.13 = (bf16[16,768]{1,0:T(8,128)(2,1)S(1)}, bf16[16,768]{1,0:T(8,128)(2,1)S(1)}, u32[]{:S(2)}, u32[]{:S(2)}) collective-permute-start(bf16[16,768]{1,0:T(8,128)(2,1)S(1)} %shard_map.88.part_ref), channel_id=1, source_target_pairs={{0,3},{1,2},{2,1},{3,0},{4,7},{5,6},{6,5},{7,4},{8,11},{9,10},{10,... | collective-permute-start | bytes 73736 | tf_op jit(solution)/shard_map/ppermute | solution.py:330
  36.4 2.6 %collective-permute-done.12.beside_ref = bf16[16,768]{1,0:T(8,128)(2,1)S(1)} collective-permute-done((bf16[16,768]{1,0:T(8,128)(2,1)S(1)}, bf16[16,768]{1,0:T(8,128)(2,1)S(1)}, u32[]{:S(2)}, u32[]{:S(2)}) %collective-permute-start.12) | collective-permute-done | bytes 24608 | tf_op jit(solution)/shard_map/ppermute | solution.py:132
  39.8 4.1 %collective-permute-done.15.refs_1_ = bf16[16,1536]{1,0:T(8,128)(2,1)S(1)} collective-permute-done((bf16[16,1536]{1,0:T(8,128)(2,1)S(1)}, bf16[16,1536]{1,0:T(8,128)(2,1)S(1)}, u32[]{:S(2)}, u32[]{:S(2)}) %collective-permute-start.15) | collective-permute-done | bytes 49184 | tf_op jit(solution)/shard_map/ppermute | solution.py:144
  44.1 2.5 %shard_map.91 = (f32[16,3072]{1,0:T(8,128)S(1)}, bf16[16,3072]{1,0:T(8,128)(2,1)S(1)}) custom-call(bf16[16,3072]{1,0:T(8,128)(2,1)S(1)} %get-tuple-element.31.left_ref, bf16[3072,3072]{1,0:T(8,128)(2,1)S(1)} %bitcast.1), custom_call_target="tpu_custom_call" | custom-call | flops 2000000000 | bytes 100000 | tf_op jit(solution)/shard_map/pallas_call | solution.py:115
  46.6 2.7 %collective-permute-start.16 = (bf16[16,3072]{1,0:T(8,128)(2,1)S(1)}, bf16[16,3072]{1,0:T(8,128)(2,1)S(1)}, u32[]{:S(2)}, u32[]{:S(2)}) collective-permute-start(bf16[16,3072]{1,0:T(8,128)(2,1)S(1)} %get-tuple-element.33), channel_id=1, source_target_pairs={{0,1},{1,0},{2,3},{3,2},{4,5},{5,4},{6,7},{7,6},{8,9},{9,8},{10,11... | collective-permute-start | bytes 294920 | tf_op jit(solution)/shard_map/ppermute | solution.py:127
  49.4 2.5 %shard_map.92 = (f32[16,3072]{1,0:T(8,128)S(1)}, bf16[16,3072]{1,0:T(8,128)(2,1)S(1)}) custom-call(bf16[16,3072]{1,0:T(8,128)(2,1)S(1)} %get-tuple-element.31.left_ref, bf16[3072,3072]{1,0:T(8,128)(2,1)S(1)} %bitcast.3), custom_call_target="tpu_custom_call" | custom-call | flops 2000000000 | bytes 100000 | tf_op jit(solution)/shard_map/pallas_call | solution.py:115
  51.9 0.8 %collective-permute-start.17 = (bf16[16,3072]{1,0:T(8,128)(2,1)S(1)}, bf16[16,3072]{1,0:T(8,128)(2,1)S(1)}, u32[]{:S(2)}, u32[]{:S(2)}) collective-permute-start(bf16[16,3072]{1,0:T(8,128)(2,1)S(1)} %get-tuple-element.35), channel_id=1, source_target_pairs={{0,1},{1,0},{2,3},{3,2},{4,5},{5,4},{6,7},{7,6},{8,9},{9,8},{10,11... | collective-permute-start | bytes 294920 | tf_op jit(solution)/shard_map/ppermute | solution.py:127
  52.8 1.1 %collective-permute-done.18.refs_5_ = f32[16,128]{1,0:T(8,128)S(1)} collective-permute-done((f32[16,128]{1,0:T(8,128)S(1)}, f32[16,128]{1,0:T(8,128)S(1)}, u32[]{:S(2)}, u32[]{:S(2)}) %collective-permute-start.18) | collective-permute-done | bytes 8224 | tf_op jit(solution)/shard_map/ppermute | solution.py:127
  54.0 2.6 %shard_map.93 = bf16[8,2,3072]{2,1,0:T(2,128)(2,1)S(1)} custom-call(f32[16,3072]{1,0:T(8,128)S(1)} %get-tuple-element.32.refs_0_, bf16[16,3072]{1,0:T(8,128)(2,1)S(1)} %collective-permute-done.16.refs_1_, f32[16,3072]{1,0:T(8,128)S(1)} %get-tuple-element.34.refs_2_, bf16[16,3072]{1,0:T(8,128)(2,1)S(1)} %collective-permute-done.17.refs_3_, ...), custom_call_target="tpu_custom_call" | custom-call | flops 2000000000 | bytes 100000 | tf_op jit(solution)/shard_map/pallas_call | solution.py:115
  56.6 10.6 %all_to_all.5.blocks_ref = bf16[8,2,3072]{2,1,0:T(2,128)(2,1)S(1)} all-to-all(bf16[8,2,3072]{2,1,0:T(2,128)(2,1)S(1)} %shard_map.93), channel_id=1, replica_groups=mesh['groups'=2,'row'=8,'col'=2] {'row'}, dimensions={0} | all-to-all | bytes 196608 | tf_op jit(solution)/shard_map/all_to_all | solution.py:352
  (74 shorter events, 6.7 us)
Async XLA Ops:
  0.0 5.1 %collective-permute-start = (bf16[2,3072]{1,0:T(2,128)(2,1)}, bf16[2,3072]{1,0:T(2,128)(2,1)S(1)}, u32[]{:S(2)}, u32[]{:S(2)}) collective-permute-start(bf16[2,3072]{1,0:T(2,128)(2,1)} %refs_0_.1), channel_id=1, source_target_pairs={{0,2},{2,0},{4,6},{6,4},{8,10},{10,8},{12,14},{14,12},{1,3},{3,1},... | collective-permute-start | bytes 36872 | tf_op jit(solution)/shard_map/ppermute | solution.py:132
  5.1 4.5 %collective-permute-start.1 = (bf16[2,2,3072]{2,1,0:T(2,128)(2,1)S(1)}, bf16[2,2,3072]{2,1,0:T(2,128)(2,1)S(1)}, u32[]{:S(2)}, u32[]{:S(2)}) collective-permute-start(bf16[2,2,3072]{2,1,0:T(2,128)(2,1)S(1)} %shard_map.83.refs_0_), channel_id=1, source_target_pairs={{0,4},{2,6},{4,0},{6,2},{8,12},{10,14},{12,8},{14,10},{1,5},{3,7},... | collective-permute-start | bytes 73736 | tf_op jit(solution)/shard_map/ppermute | solution.py:132
  6.9 4.8 %collective-permute-start.2 = (bf16[2,2,3072]{2,1,0:T(2,128)(2,1)S(1)}, bf16[2,2,3072]{2,1,0:T(2,128)(2,1)S(1)}, u32[]{:S(2)}, u32[]{:S(2)}) collective-permute-start(bf16[2,2,3072]{2,1,0:T(2,128)(2,1)S(1)} %shard_map.83.refs_0_), channel_id=1, source_target_pairs={{0,8},{2,10},{4,12},{6,14},{8,0},{10,2},{12,4},{14,6},{1,9},{3,11}... | collective-permute-start | bytes 73736 | tf_op jit(solution)/shard_map/ppermute | solution.py:132
  9.5 5.6 %collective-permute-start.3 = (bf16[2,2,3072]{2,1,0:T(2,128)(2,1)S(1)}, bf16[2,2,3072]{2,1,0:T(2,128)(2,1)S(1)}, u32[]{:S(2)}, u32[]{:S(2)}) collective-permute-start(bf16[2,2,3072]{2,1,0:T(2,128)(2,1)S(1)} %shard_map.83.refs_0_), channel_id=1, source_target_pairs={{0,12},{2,14},{4,8},{6,10},{8,4},{10,6},{12,0},{14,2},{1,13},{3,15... | collective-permute-start | bytes 73736 | tf_op jit(solution)/shard_map/ppermute | solution.py:132
  15.3 28.5 %copy-start.3 = (f32[3072]{0:T(1024)S(1)}, f32[3072]{0:T(1024)}, u32[]{:S(2)}) copy-start(f32[3072]{0:T(1024)} %refs_3_.1) | copy-start | bytes 36868
  15.4 28.6 %slice-start = ((s8[18874368]{0:T(1024)(128)(4,1)}), s8[4194304]{0:T(1024)(128)(4,1)S(1)}, s32[]{:S(2)}) async-start(s8[18874368]{0:T(1024)(128)(4,1)} %bitcast), calls=%async_computation.1 | async-start | bytes 8388608
  15.4 28.6 %slice-start.1 = ((s8[18874368]{0:T(1024)(128)(4,1)}), s8[4194304]{0:T(1024)(128)(4,1)S(1)}, s32[]{:S(2)}) async-start(s8[18874368]{0:T(1024)(128)(4,1)} %bitcast), calls=%async_computation.2 | async-start | bytes 8388608
  17.3 1.4 %collective-permute-start.4 = (bf16[16,2304]{1,0:T(8,128)(2,1)S(1)}, bf16[16,2304]{1,0:T(8,128)(2,1)S(1)}, u32[]{:S(2)}, u32[]{:S(2)}) collective-permute-start(bf16[16,2304]{1,0:T(8,128)(2,1)S(1)} %get-tuple-element.25), channel_id=1, source_target_pairs={{0,1},{1,0},{2,3},{3,2},{4,5},{5,4},{6,7},{7,6},{8,9},{9,8},{10,11... | collective-permute-start | bytes 221192 | tf_op jit(solution)/shard_map/ppermute | solution.py:127
  17.3 1.3 %collective-permute-start.5 = (f32[16,128]{1,0:T(8,128)S(1)}, f32[16,128]{1,0:T(8,128)S(1)}, u32[]{:S(2)}, u32[]{:S(2)}) collective-permute-start(f32[16,128]{1,0:T(8,128)S(1)} %get-tuple-element.26.squares_ref), channel_id=1, source_target_pairs={{0,1},{1,0},{2,3},{3,2},{4,5},{5,4},{6,7},{7,6},{8,9},{9,8},{10,11... | collective-permute-start | bytes 24584 | tf_op jit(solution)/shard_map/ppermute | solution.py:127
  18.7 30.7 %slice-start.5 = ((s8[18874368]{0:T(1024)(128)(4,1)}), s8[2097152]{0:T(1024)(128)(4,1)S(1)}, s32[]{:S(2)}) async-start(s8[18874368]{0:T(1024)(128)(4,1)} %bitcast.2), calls=%async_computation.6 | async-start | bytes 4194304
  18.8 6.3 %collective-permute-start.6 = (bf16[16,1536]{1,0:T(8,128)(2,1)S(1)}, bf16[16,1536]{1,0:T(8,128)(2,1)S(1)}, u32[]{:S(2)}, u32[]{:S(2)}) collective-permute-start(bf16[16,1536]{1,0:T(8,128)(2,1)S(1)} %get-tuple-element.27.kept_ref), channel_id=1, source_target_pairs={{0,2},{2,0},{4,6},{6,4},{8,10},{10,8},{12,14},{14,12},{1,3},{3,1},... | collective-permute-start | bytes 147464 | tf_op jit(solution)/shard_map/ppermute | solution.py:132
  20.3 29.0 %slice-start.6 = ((s8[18874368]{0:T(1024)(128)(4,1)}), s8[4194304]{0:T(1024)(128)(4,1)S(1)}, s32[]{:S(2)}) async-start(s8[18874368]{0:T(1024)(128)(4,1)} %bitcast.2), calls=%async_computation.7 | async-start | bytes 8388608
  20.3 3.8 %collective-permute-start.7 = (bf16[16,768]{1,0:T(8,128)(2,1)S(1)}, bf16[16,768]{1,0:T(8,128)(2,1)S(1)}, u32[]{:S(2)}, u32[]{:S(2)}) collective-permute-start(bf16[16,768]{1,0:T(8,128)(2,1)S(1)} %get-tuple-element.28), channel_id=1, source_target_pairs={{0,4},{2,6},{4,0},{6,2},{8,12},{10,14},{12,8},{14,10},{1,5},{3,7},... | collective-permute-start | bytes 73736 | tf_op jit(solution)/shard_map/ppermute | solution.py:132
  20.3 4.7 %collective-permute-start.8 = (bf16[16,768]{1,0:T(8,128)(2,1)S(1)}, bf16[16,768]{1,0:T(8,128)(2,1)S(1)}, u32[]{:S(2)}, u32[]{:S(2)}) collective-permute-start(bf16[16,768]{1,0:T(8,128)(2,1)S(1)} %get-tuple-element.28), channel_id=1, source_target_pairs={{0,6},{2,4},{4,2},{6,0},{8,14},{10,12},{12,10},{14,8},{1,7},{3,5},... | collective-permute-start | bytes 73736 | tf_op jit(solution)/shard_map/ppermute | solution.py:132
  25.7 2.9 %collective-permute-start.9 = (bf16[16,1536]{1,0:T(8,128)(2,1)S(1)}, bf16[16,1536]{1,0:T(8,128)(2,1)S(1)}, u32[]{:S(2)}, u32[]{:S(2)}) collective-permute-start(bf16[16,1536]{1,0:T(8,128)(2,1)S(1)} %shard_map.87.own_ref), channel_id=1, source_target_pairs={{1,8},{3,10},{5,12},{7,14},{8,1},{10,3},{12,5},{14,7},{17,24},{19,... | collective-permute-start | bytes 147464 | tf_op jit(solution)/shard_map/ppermute | solution.py:144
  26.5 4.2 %collective-permute-start.10 = (bf16[16,1536]{1,0:T(8,128)(2,1)S(1)}, bf16[16,1536]{1,0:T(8,128)(2,1)S(1)}, u32[]{:S(2)}, u32[]{:S(2)}) collective-permute-start(bf16[16,1536]{1,0:T(8,128)(2,1)S(1)} %shard_map.87.own_ref), channel_id=1, source_target_pairs={{0,4},{1,12},{2,6},{3,14},{4,0},{5,8},{6,2},{7,10},{9,13},{8,5},{1... | collective-permute-start | bytes 147464 | tf_op jit(solution)/shard_map/ppermute | solution.py:144
  31.4 5.0 %collective-permute-start.11 = (bf16[16,768]{1,0:T(8,128)(2,1)S(1)}, bf16[16,768]{1,0:T(8,128)(2,1)S(1)}, u32[]{:S(2)}, u32[]{:S(2)}) collective-permute-start(bf16[16,768]{1,0:T(8,128)(2,1)S(1)} %shard_map.88.part_ref), channel_id=1, source_target_pairs={{0,1},{1,0},{2,3},{3,2},{4,5},{5,4},{6,7},{7,6},{8,9},{9,8},{10,11... | collective-permute-start | bytes 73736 | tf_op jit(solution)/shard_map/ppermute | solution.py:127
  35.0 4.0 %collective-permute-start.12 = (bf16[16,768]{1,0:T(8,128)(2,1)S(1)}, bf16[16,768]{1,0:T(8,128)(2,1)S(1)}, u32[]{:S(2)}, u32[]{:S(2)}) collective-permute-start(bf16[16,768]{1,0:T(8,128)(2,1)S(1)} %shard_map.88.part_ref), channel_id=1, source_target_pairs={{0,2},{2,0},{4,6},{6,4},{8,10},{10,8},{12,14},{14,12},{1,3},{3,1},... | collective-permute-start | bytes 73736 | tf_op jit(solution)/shard_map/ppermute | solution.py:132
  35.5 3.5 %collective-permute-start.13 = (bf16[16,768]{1,0:T(8,128)(2,1)S(1)}, bf16[16,768]{1,0:T(8,128)(2,1)S(1)}, u32[]{:S(2)}, u32[]{:S(2)}) collective-permute-start(bf16[16,768]{1,0:T(8,128)(2,1)S(1)} %shard_map.88.part_ref), channel_id=1, source_target_pairs={{0,3},{1,2},{2,1},{3,0},{4,7},{5,6},{6,5},{7,4},{8,11},{9,10},{10,... | collective-permute-start | bytes 73736 | tf_op jit(solution)/shard_map/ppermute | solution.py:330
  39.0 0.8 %collective-permute-start.14 = (bf16[16,1536]{1,0:T(8,128)(2,1)S(1)}, bf16[16,1536]{1,0:T(8,128)(2,1)S(1)}, u32[]{:S(2)}, u32[]{:S(2)}) collective-permute-start(bf16[16,1536]{1,0:T(8,128)(2,1)S(1)} %shard_map.89.own_ref), channel_id=1, source_target_pairs={{1,8},{3,10},{5,12},{7,14},{8,1},{10,3},{12,5},{14,7},{17,24},{19,... | collective-permute-start | bytes 147464 | tf_op jit(solution)/shard_map/ppermute | solution.py:144
  39.7 4.2 %collective-permute-start.15 = (bf16[16,1536]{1,0:T(8,128)(2,1)S(1)}, bf16[16,1536]{1,0:T(8,128)(2,1)S(1)}, u32[]{:S(2)}, u32[]{:S(2)}) collective-permute-start(bf16[16,1536]{1,0:T(8,128)(2,1)S(1)} %shard_map.89.own_ref), channel_id=1, source_target_pairs={{0,4},{1,12},{2,6},{3,14},{4,0},{5,8},{6,2},{7,10},{9,13},{8,5},{1... | collective-permute-start | bytes 147464 | tf_op jit(solution)/shard_map/ppermute | solution.py:144
  46.6 7.3 %collective-permute-start.16 = (bf16[16,3072]{1,0:T(8,128)(2,1)S(1)}, bf16[16,3072]{1,0:T(8,128)(2,1)S(1)}, u32[]{:S(2)}, u32[]{:S(2)}) collective-permute-start(bf16[16,3072]{1,0:T(8,128)(2,1)S(1)} %get-tuple-element.33), channel_id=1, source_target_pairs={{0,1},{1,0},{2,3},{3,2},{4,5},{5,4},{6,7},{7,6},{8,9},{9,8},{10,11... | collective-permute-start | bytes 294920 | tf_op jit(solution)/shard_map/ppermute | solution.py:127
  51.9 2.0 %collective-permute-start.17 = (bf16[16,3072]{1,0:T(8,128)(2,1)S(1)}, bf16[16,3072]{1,0:T(8,128)(2,1)S(1)}, u32[]{:S(2)}, u32[]{:S(2)}) collective-permute-start(bf16[16,3072]{1,0:T(8,128)(2,1)S(1)} %get-tuple-element.35), channel_id=1, source_target_pairs={{0,1},{1,0},{2,3},{3,2},{4,5},{5,4},{6,7},{7,6},{8,9},{9,8},{10,11... | collective-permute-start | bytes 294920 | tf_op jit(solution)/shard_map/ppermute | solution.py:127
  52.8 1.2 %collective-permute-start.18 = (f32[16,128]{1,0:T(8,128)S(1)}, f32[16,128]{1,0:T(8,128)S(1)}, u32[]{:S(2)}, u32[]{:S(2)}) collective-permute-start(f32[16,128]{1,0:T(8,128)S(1)} %get-tuple-element.36.refs_4_), channel_id=1, source_target_pairs={{0,1},{1,0},{2,3},{3,2},{4,5},{5,4},{6,7},{7,6},{8,9},{9,8},{10,11... | collective-permute-start | bytes 24584 | tf_op jit(solution)/shard_map/ppermute | solution.py:127
  (16 other events, 233.0 us)

commit v5 on v4

--- a/solution.py
+++ b/solution.py
@@ -167,17 +167,21 @@
         target[...] = source[...]
 
 
-def pair_kernel(mine_ref, other_ref, both_ref):
-    both_ref[0] = mine_ref[...]
-    both_ref[1] = other_ref[...]
+def scale_kernel(scale_ref, _, brought_ref):
+    brought_ref[...] = scale_ref[...]
+
+
+def pair_kernel(*refs):
+    for place, ref in enumerate(refs[:-1]):
+        refs[-1][place] = ref[...]
 
 
 def enter_kernel(*refs):
-    pairs, (scale_ref, stream_ref, scaled_ref, squares_ref, blocks) = refs[:4], refs[4:]
+    columns, (scale_ref, stream_ref, scaled_ref, squares_ref, blocks) = refs[:2], refs[2:]
     mine = lax.axis_index("row")
-    for step, pair_ref in enumerate(pairs):
-        for near in range(2):
-            blocks[mine ^ (2 * step + near)] = pair_ref[near].astype(jnp.float32)
+    for near, column_ref in enumerate(columns):
+        for step in range(column_ref.shape[0]):
+            blocks[mine ^ (2 * step + near)] = column_ref[step].astype(jnp.float32)
     count, rows, _ = blocks.shape
     for block in range(count):
         stream_ref[rows * block : rows * (block + 1)] = blocks[block]
@@ -305,11 +309,11 @@
     count = lax.axis_size("row")
     tokens = tok_rows * count
 
-    beside = from_row(hidden_states, 1)
-    held = (hidden_states, scale_attn)
-    own, scale_attn = call(bring_kernel, [(v.shape, v.dtype) for v in held], *held)
-    [pair] = call(pair_kernel, [((2, tok_rows, half), bf16)], own, beside)
-    pairs = [pair] + [from_row(pair, 2 * step) for step in range(1, count // 2)]
+    along = [from_row(hidden_states, 2 * step) for step in range(1, count // 2)]
+    [own] = call(bring_kernel, [(hidden_states.shape, bf16)], hidden_states)
+    [column] = call(pair_kernel, [((count // 2, tok_rows, half), bf16)], own, *along)
+    pairs = [column, from_row(column, 1)]
+    [scale_attn] = call(scale_kernel, [(scale_attn.shape, f32)], scale_attn, column)
     stream, scaled, squares = call(
         enter_kernel,
         [((tokens, half), f32), ((tokens, half), bf16), ((tokens, 128), f32)],

time: 68.2 us -> 68.4 us (level)
  waiting for transfers between devices: 19.1 us -> 20.2 us
  local copies, waits for them, and re-layouts: 2.26 us -> 1.57 us
    ppermute x8, waiting for transfers between devices: 10.9 us -> 12.1 us  [from_row(): return lax.ppermute(block, 'row', [(i, i ^ step) for i in range(count)])]
    unnamed x42, local copies, waits for them, and re-layouts: 2.26 us -> 1.57 us
    pallas_call x13 -> x14, Pallas kernels: 12 us -> 12 us  [call(): pl.pallas_call(kernel, out_shape=[jax.ShapeDtypeStruct(*out) for out in o...]
  transfers between devices with their start and end apart: 19 -> 19, of which waited for: 9 -> 10; matrix products, arithmetic and copies ran while one was open for 0% -> 0% of each run, Pallas kernels for 4% -> 4%
where the time goes in v5:
time: 68.4 us; the launch traced here: 68.1 us
  starting transfers between devices  23.2 us (34%)
  waiting for transfers between devices  20.2 us (30%)
  Pallas kernels  12 us (18%)
  blocking collectives  10.8 us (16%)
  local copies, waits for them, and re-layouts  1.57 us (2%)
    ppermute x8, waiting for transfers between devices, from_row(): return lax.ppermute(block, 'row', [(i, i ^ step) for i in range(count)])  12.1 us
    pallas_call x14, Pallas kernels, call(): pl.pallas_call(kernel, out_shape=[jax.ShapeDtypeStruct(*out) for out in o...  12 us
    ppermute x8, starting transfers between devices, from_row(): return lax.ppermute(block, 'row', [(i, i ^ step) for i in range(count)])  11.1 us
    all_to_all x1, blocking collectives, few_rows(): lax.all_to_all(lowered, 'row', split_axis=0, concat_axis=0, tiled=True)  10.8 us
    ppermute x6, starting transfers between devices, other_core(): return lax.ppermute(block, 'col', [(0, 1), (1, 0)])  7.57 us
    ppermute x4, waiting for transfers between devices, spread(): got.append(lax.ppermute(block, ('row', 'col'), pairs))  6.14 us
    ppermute x4, starting transfers between devices, spread(): got.append(lax.ppermute(block, ('row', 'col'), pairs))  3.61 us
    ppermute x6, waiting for transfers between devices, other_core(): return lax.ppermute(block, 'col', [(0, 1), (1, 0)])  1.98 us
  transfers between devices with their start and end apart: 19, of which 10 were waited for; matrix products, arithmetic and copies ran while one was open for 0% of the time, Pallas kernels for 4%

profile of v5, /device:TPU:0, one launch (start us, length us, event | category | flops | bytes accessed | tf_op | source)
XLA Modules:
  0.0 68.1 jit_solution(11242986264634557593)
XLA Ops:
  0.0 3.0 %collective-permute-start = (bf16[2,3072]{1,0:T(2,128)(2,1)}, bf16[2,3072]{1,0:T(2,128)(2,1)S(1)}, u32[]{:S(2)}, u32[]{:S(2)}) collective-permute-start(bf16[2,3072]{1,0:T(2,128)(2,1)} %refs_0_.1), channel_id=1, source_target_pairs={{0,4},{2,6},{4,0},{6,2},{8,12},{10,14},{12,8},{14,10},{1,5},{3,7},... | collective-permute-start | bytes 36872 | tf_op jit(solution)/shard_map/ppermute | solution.py:132
  3.0 2.6 %collective-permute-start.1 = (bf16[2,3072]{1,0:T(2,128)(2,1)}, bf16[2,3072]{1,0:T(2,128)(2,1)S(1)}, u32[]{:S(2)}, u32[]{:S(2)}) collective-permute-start(bf16[2,3072]{1,0:T(2,128)(2,1)} %refs_0_.1), channel_id=1, source_target_pairs={{0,8},{2,10},{4,12},{6,14},{8,0},{10,2},{12,4},{14,6},{1,9},{3,11}... | collective-permute-start | bytes 36872 | tf_op jit(solution)/shard_map/ppermute | solution.py:132
  6.4 1.4 %collective-permute-done.1.refs_2_ = bf16[2,3072]{1,0:T(2,128)(2,1)S(1)} collective-permute-done((bf16[2,3072]{1,0:T(2,128)(2,1)}, bf16[2,3072]{1,0:T(2,128)(2,1)S(1)}, u32[]{:S(2)}, u32[]{:S(2)}) %collective-permute-start.1) | collective-permute-done | bytes 12320 | tf_op jit(solution)/shard_map/ppermute | solution.py:132
  7.8 3.5 %collective-permute-done.2.refs_3_ = bf16[2,3072]{1,0:T(2,128)(2,1)S(1)} collective-permute-done((bf16[2,3072]{1,0:T(2,128)(2,1)}, bf16[2,3072]{1,0:T(2,128)(2,1)S(1)}, u32[]{:S(2)}, u32[]{:S(2)}) %collective-permute-start.2) | collective-permute-done | bytes 12320 | tf_op jit(solution)/shard_map/ppermute | solution.py:132
  11.3 1.5 %collective-permute-start.3 = (bf16[4,2,3072]{2,1,0:T(2,128)(2,1)S(1)}, bf16[4,2,3072]{2,1,0:T(2,128)(2,1)S(1)}, u32[]{:S(2)}, u32[]{:S(2)}) collective-permute-start(bf16[4,2,3072]{2,1,0:T(2,128)(2,1)S(1)} %shard_map.83._.refs_0_), channel_id=1, source_target_pairs={{0,2},{2,0},{4,6},{6,4},{8,10},{10,8},{12,14},{14,12},{1,3},{3,1},... | collective-permute-start | bytes 147464 | tf_op jit(solution)/shard_map/ppermute | solution.py:132
  13.5 1.9 %collective-permute-done.3.refs_1_ = bf16[4,2,3072]{2,1,0:T(2,128)(2,1)S(1)} collective-permute-done((bf16[4,2,3072]{2,1,0:T(2,128)(2,1)S(1)}, bf16[4,2,3072]{2,1,0:T(2,128)(2,1)S(1)}, u32[]{:S(2)}, u32[]{:S(2)}) %collective-permute-start.3) | collective-permute-done | bytes 49184 | tf_op jit(solution)/shard_map/ppermute | solution.py:132
  15.6 1.9 %shard_map.86 = (f32[16,2304]{1,0:T(8,128)S(1)}, bf16[16,2304]{1,0:T(8,128)(2,1)S(1)}) custom-call(bf16[16,3072]{1,0:T(8,128)(2,1)S(1)} %get-tuple-element.19.left_ref, bf16[3072,2304]{1,0:T(8,128)(2,1)S(1)} %copy-done), custom_call_target="tpu_custom_call" | custom-call | flops 2000000000 | bytes 100000 | tf_op jit(solution)/shard_map/pallas_call | solution.py:115
  19.0 1.6 %collective-permute-start.6 = (bf16[16,1536]{1,0:T(8,128)(2,1)S(1)}, bf16[16,1536]{1,0:T(8,128)(2,1)S(1)}, u32[]{:S(2)}, u32[]{:S(2)}) collective-permute-start(bf16[16,1536]{1,0:T(8,128)(2,1)S(1)} %get-tuple-element.23.kept_ref), channel_id=1, source_target_pairs={{0,2},{2,0},{4,6},{6,4},{8,10},{10,8},{12,14},{14,12},{1,3},{3,1},... | collective-permute-start | bytes 147464 | tf_op jit(solution)/shard_map/ppermute | solution.py:132
  20.6 2.0 %collective-permute-start.8 = (bf16[16,768]{1,0:T(8,128)(2,1)S(1)}, bf16[16,768]{1,0:T(8,128)(2,1)S(1)}, u32[]{:S(2)}, u32[]{:S(2)}) collective-permute-start(bf16[16,768]{1,0:T(8,128)(2,1)S(1)} %get-tuple-element.24), channel_id=1, source_target_pairs={{0,6},{2,4},{4,2},{6,0},{8,14},{10,12},{12,10},{14,8},{1,7},{3,5},... | collective-permute-start | bytes 73736 | tf_op jit(solution)/shard_map/ppermute | solution.py:132
  22.6 1.8 %collective-permute-done.7.straight_ref = bf16[16,768]{1,0:T(8,128)(2,1)S(1)} collective-permute-done((bf16[16,768]{1,0:T(8,128)(2,1)S(1)}, bf16[16,768]{1,0:T(8,128)(2,1)S(1)}, u32[]{:S(2)}, u32[]{:S(2)}) %collective-permute-start.7) | collective-permute-done | bytes 24608 | tf_op jit(solution)/shard_map/ppermute | solution.py:132
  24.4 0.9 %collective-permute-done.8.across_ref = bf16[16,768]{1,0:T(8,128)(2,1)S(1)} collective-permute-done((bf16[16,768]{1,0:T(8,128)(2,1)S(1)}, bf16[16,768]{1,0:T(8,128)(2,1)S(1)}, u32[]{:S(2)}, u32[]{:S(2)}) %collective-permute-start.8) | collective-permute-done | bytes 24608 | tf_op jit(solution)/shard_map/ppermute | solution.py:132
  26.8 2.1 %collective-permute-start.10 = (bf16[16,1536]{1,0:T(8,128)(2,1)S(1)}, bf16[16,1536]{1,0:T(8,128)(2,1)S(1)}, u32[]{:S(2)}, u32[]{:S(2)}) collective-permute-start(bf16[16,1536]{1,0:T(8,128)(2,1)S(1)} %shard_map.88.own_ref), channel_id=1, source_target_pairs={{0,4},{1,12},{2,6},{3,14},{4,0},{5,8},{6,2},{7,10},{9,13},{8,5},{1... | collective-permute-start | bytes 147464 | tf_op jit(solution)/shard_map/ppermute | solution.py:144
  28.8 2.1 %collective-permute-done.10.refs_1_ = bf16[16,1536]{1,0:T(8,128)(2,1)S(1)} collective-permute-done((bf16[16,1536]{1,0:T(8,128)(2,1)S(1)}, bf16[16,1536]{1,0:T(8,128)(2,1)S(1)}, u32[]{:S(2)}, u32[]{:S(2)}) %collective-permute-start.10) | collective-permute-done | bytes 49184 | tf_op jit(solution)/shard_map/ppermute | solution.py:144
  31.7 3.5 %collective-permute-start.11 = (bf16[16,768]{1,0:T(8,128)(2,1)S(1)}, bf16[16,768]{1,0:T(8,128)(2,1)S(1)}, u32[]{:S(2)}, u32[]{:S(2)}) collective-permute-start(bf16[16,768]{1,0:T(8,128)(2,1)S(1)} %shard_map.89.part_ref), channel_id=1, source_target_pairs={{0,1},{1,0},{2,3},{3,2},{4,5},{5,4},{6,7},{7,6},{8,9},{9,8},{10,11... | collective-permute-start | bytes 73736 | tf_op jit(solution)/shard_map/ppermute | solution.py:127
  35.6 1.0 %collective-permute-start.13 = (bf16[16,768]{1,0:T(8,128)(2,1)S(1)}, bf16[16,768]{1,0:T(8,128)(2,1)S(1)}, u32[]{:S(2)}, u32[]{:S(2)}) collective-permute-start(bf16[16,768]{1,0:T(8,128)(2,1)S(1)} %shard_map.89.part_ref), channel_id=1, source_target_pairs={{0,3},{1,2},{2,1},{3,0},{4,7},{5,6},{6,5},{7,4},{8,11},{9,10},{10,... | collective-permute-start | bytes 73736 | tf_op jit(solution)/shard_map/ppermute | solution.py:334
  36.6 2.5 %collective-permute-done.12.beside_ref = bf16[16,768]{1,0:T(8,128)(2,1)S(1)} collective-permute-done((bf16[16,768]{1,0:T(8,128)(2,1)S(1)}, bf16[16,768]{1,0:T(8,128)(2,1)S(1)}, u32[]{:S(2)}, u32[]{:S(2)}) %collective-permute-start.12) | collective-permute-done | bytes 24608 | tf_op jit(solution)/shard_map/ppermute | solution.py:132
  39.9 4.1 %collective-permute-done.15.refs_1_ = bf16[16,1536]{1,0:T(8,128)(2,1)S(1)} collective-permute-done((bf16[16,1536]{1,0:T(8,128)(2,1)S(1)}, bf16[16,1536]{1,0:T(8,128)(2,1)S(1)}, u32[]{:S(2)}, u32[]{:S(2)}) %collective-permute-start.15) | collective-permute-done | bytes 49184 | tf_op jit(solution)/shard_map/ppermute | solution.py:144
  44.2 2.5 %shard_map.92 = (f32[16,3072]{1,0:T(8,128)S(1)}, bf16[16,3072]{1,0:T(8,128)(2,1)S(1)}) custom-call(bf16[16,3072]{1,0:T(8,128)(2,1)S(1)} %get-tuple-element.27.left_ref, bf16[3072,3072]{1,0:T(8,128)(2,1)S(1)} %bitcast.1), custom_call_target="tpu_custom_call" | custom-call | flops 2000000000 | bytes 100000 | tf_op jit(solution)/shard_map/pallas_call | solution.py:115
  46.7 2.7 %collective-permute-start.16 = (bf16[16,3072]{1,0:T(8,128)(2,1)S(1)}, bf16[16,3072]{1,0:T(8,128)(2,1)S(1)}, u32[]{:S(2)}, u32[]{:S(2)}) collective-permute-start(bf16[16,3072]{1,0:T(8,128)(2,1)S(1)} %get-tuple-element.29), channel_id=1, source_target_pairs={{0,1},{1,0},{2,3},{3,2},{4,5},{5,4},{6,7},{7,6},{8,9},{9,8},{10,11... | collective-permute-start | bytes 294920 | tf_op jit(solution)/shard_map/ppermute | solution.py:127
  49.4 2.5 %shard_map.93 = (f32[16,3072]{1,0:T(8,128)S(1)}, bf16[16,3072]{1,0:T(8,128)(2,1)S(1)}) custom-call(bf16[16,3072]{1,0:T(8,128)(2,1)S(1)} %get-tuple-element.27.left_ref, bf16[3072,3072]{1,0:T(8,128)(2,1)S(1)} %bitcast.3), custom_call_target="tpu_custom_call" | custom-call | flops 2000000000 | bytes 100000 | tf_op jit(solution)/shard_map/pallas_call | solution.py:115
  52.0 0.8 %collective-permute-start.17 = (bf16[16,3072]{1,0:T(8,128)(2,1)S(1)}, bf16[16,3072]{1,0:T(8,128)(2,1)S(1)}, u32[]{:S(2)}, u32[]{:S(2)}) collective-permute-start(bf16[16,3072]{1,0:T(8,128)(2,1)S(1)} %get-tuple-element.31), channel_id=1, source_target_pairs={{0,1},{1,0},{2,3},{3,2},{4,5},{5,4},{6,7},{7,6},{8,9},{9,8},{10,11... | collective-permute-start | bytes 294920 | tf_op jit(solution)/shard_map/ppermute | solution.py:127
  52.9 1.1 %collective-permute-done.18.refs_5_ = f32[16,128]{1,0:T(8,128)S(1)} collective-permute-done((f32[16,128]{1,0:T(8,128)S(1)}, f32[16,128]{1,0:T(8,128)S(1)}, u32[]{:S(2)}, u32[]{:S(2)}) %collective-permute-start.18) | collective-permute-done | bytes 8224 | tf_op jit(solution)/shard_map/ppermute | solution.py:127
  54.1 2.6 %shard_map.94 = bf16[8,2,3072]{2,1,0:T(2,128)(2,1)S(1)} custom-call(f32[16,3072]{1,0:T(8,128)S(1)} %get-tuple-element.28.refs_0_, bf16[16,3072]{1,0:T(8,128)(2,1)S(1)} %collective-permute-done.16.refs_1_, f32[16,3072]{1,0:T(8,128)S(1)} %get-tuple-element.30.refs_2_, bf16[16,3072]{1,0:T(8,128)(2,1)S(1)} %collective-permute-done.17.refs_3_, ...), custom_call_target="tpu_custom_call" | custom-call | flops 2000000000 | bytes 100000 | tf_op jit(solution)/shard_map/pallas_call | solution.py:115
  56.7 10.8 %all_to_all.5.blocks_ref = bf16[8,2,3072]{2,1,0:T(2,128)(2,1)S(1)} all-to-all(bf16[8,2,3072]{2,1,0:T(2,128)(2,1)S(1)} %shard_map.94), channel_id=1, replica_groups=mesh['groups'=2,'row'=8,'col'=2] {'row'}, dimensions={0} | all-to-all | bytes 196608 | tf_op jit(solution)/shard_map/all_to_all | solution.py:356
  (75 shorter events, 7.3 us)
Async XLA Ops:
  0.0 6.4 %collective-permute-start = (bf16[2,3072]{1,0:T(2,128)(2,1)}, bf16[2,3072]{1,0:T(2,128)(2,1)S(1)}, u32[]{:S(2)}, u32[]{:S(2)}) collective-permute-start(bf16[2,3072]{1,0:T(2,128)(2,1)} %refs_0_.1), channel_id=1, source_target_pairs={{0,4},{2,6},{4,0},{6,2},{8,12},{10,14},{12,8},{14,10},{1,5},{3,7},... | collective-permute-start | bytes 36872 | tf_op jit(solution)/shard_map/ppermute | solution.py:132
  3.0 4.8 %collective-permute-start.1 = (bf16[2,3072]{1,0:T(2,128)(2,1)}, bf16[2,3072]{1,0:T(2,128)(2,1)S(1)}, u32[]{:S(2)}, u32[]{:S(2)}) collective-permute-start(bf16[2,3072]{1,0:T(2,128)(2,1)} %refs_0_.1), channel_id=1, source_target_pairs={{0,8},{2,10},{4,12},{6,14},{8,0},{10,2},{12,4},{14,6},{1,9},{3,11}... | collective-permute-start | bytes 36872 | tf_op jit(solution)/shard_map/ppermute | solution.py:132
  5.6 5.7 %collective-permute-start.2 = (bf16[2,3072]{1,0:T(2,128)(2,1)}, bf16[2,3072]{1,0:T(2,128)(2,1)S(1)}, u32[]{:S(2)}, u32[]{:S(2)}) collective-permute-start(bf16[2,3072]{1,0:T(2,128)(2,1)} %refs_0_.1), channel_id=1, source_target_pairs={{0,12},{2,14},{4,8},{6,10},{8,4},{10,6},{12,0},{14,2},{1,13},{3,15... | collective-permute-start | bytes 36872 | tf_op jit(solution)/shard_map/ppermute | solution.py:132
  11.3 4.1 %collective-permute-start.3 = (bf16[4,2,3072]{2,1,0:T(2,128)(2,1)S(1)}, bf16[4,2,3072]{2,1,0:T(2,128)(2,1)S(1)}, u32[]{:S(2)}, u32[]{:S(2)}) collective-permute-start(bf16[4,2,3072]{2,1,0:T(2,128)(2,1)S(1)} %shard_map.83._.refs_0_), channel_id=1, source_target_pairs={{0,2},{2,0},{4,6},{6,4},{8,10},{10,8},{12,14},{14,12},{1,3},{3,1},... | collective-permute-start | bytes 147464 | tf_op jit(solution)/shard_map/ppermute | solution.py:132
  15.6 28.4 %copy-start.3 = (f32[3072]{0:T(1024)S(1)}, f32[3072]{0:T(1024)}, u32[]{:S(2)}) copy-start(f32[3072]{0:T(1024)} %refs_3_.1) | copy-start | bytes 36868
  15.6 28.5 %slice-start = ((s8[18874368]{0:T(1024)(128)(4,1)}), s8[4194304]{0:T(1024)(128)(4,1)S(1)}, s32[]{:S(2)}) async-start(s8[18874368]{0:T(1024)(128)(4,1)} %bitcast), calls=%async_computation.1 | async-start | bytes 8388608
  15.6 28.5 %slice-start.1 = ((s8[18874368]{0:T(1024)(128)(4,1)}), s8[4194304]{0:T(1024)(128)(4,1)S(1)}, s32[]{:S(2)}) async-start(s8[18874368]{0:T(1024)(128)(4,1)} %bitcast), calls=%async_computation.2 | async-start | bytes 8388608
  17.6 1.4 %collective-permute-start.4 = (bf16[16,2304]{1,0:T(8,128)(2,1)S(1)}, bf16[16,2304]{1,0:T(8,128)(2,1)S(1)}, u32[]{:S(2)}, u32[]{:S(2)}) collective-permute-start(bf16[16,2304]{1,0:T(8,128)(2,1)S(1)} %get-tuple-element.21), channel_id=1, source_target_pairs={{0,1},{1,0},{2,3},{3,2},{4,5},{5,4},{6,7},{7,6},{8,9},{9,8},{10,11... | collective-permute-start | bytes 221192 | tf_op jit(solution)/shard_map/ppermute | solution.py:127
  17.6 1.3 %collective-permute-start.5 = (f32[16,128]{1,0:T(8,128)S(1)}, f32[16,128]{1,0:T(8,128)S(1)}, u32[]{:S(2)}, u32[]{:S(2)}) collective-permute-start(f32[16,128]{1,0:T(8,128)S(1)} %get-tuple-element.22.squares_ref), channel_id=1, source_target_pairs={{0,1},{1,0},{2,3},{3,2},{4,5},{5,4},{6,7},{7,6},{8,9},{9,8},{10,11... | collective-permute-start | bytes 24584 | tf_op jit(solution)/shard_map/ppermute | solution.py:127
  18.9 30.5 %slice-start.5 = ((s8[18874368]{0:T(1024)(128)(4,1)}), s8[2097152]{0:T(1024)(128)(4,1)S(1)}, s32[]{:S(2)}) async-start(s8[18874368]{0:T(1024)(128)(4,1)} %bitcast.2), calls=%async_computation.6 | async-start | bytes 4194304
  19.0 6.3 %collective-permute-start.6 = (bf16[16,1536]{1,0:T(8,128)(2,1)S(1)}, bf16[16,1536]{1,0:T(8,128)(2,1)S(1)}, u32[]{:S(2)}, u32[]{:S(2)}) collective-permute-start(bf16[16,1536]{1,0:T(8,128)(2,1)S(1)} %get-tuple-element.23.kept_ref), channel_id=1, source_target_pairs={{0,2},{2,0},{4,6},{6,4},{8,10},{10,8},{12,14},{14,12},{1,3},{3,1},... | collective-permute-start | bytes 147464 | tf_op jit(solution)/shard_map/ppermute | solution.py:132
  20.6 28.8 %slice-start.6 = ((s8[18874368]{0:T(1024)(128)(4,1)}), s8[4194304]{0:T(1024)(128)(4,1)S(1)}, s32[]{:S(2)}) async-start(s8[18874368]{0:T(1024)(128)(4,1)} %bitcast.2), calls=%async_computation.7 | async-start | bytes 8388608
  20.6 3.8 %collective-permute-start.7 = (bf16[16,768]{1,0:T(8,128)(2,1)S(1)}, bf16[16,768]{1,0:T(8,128)(2,1)S(1)}, u32[]{:S(2)}, u32[]{:S(2)}) collective-permute-start(bf16[16,768]{1,0:T(8,128)(2,1)S(1)} %get-tuple-element.24), channel_id=1, source_target_pairs={{0,4},{2,6},{4,0},{6,2},{8,12},{10,14},{12,8},{14,10},{1,5},{3,7},... | collective-permute-start | bytes 73736 | tf_op jit(solution)/shard_map/ppermute | solution.py:132
  20.6 4.7 %collective-permute-start.8 = (bf16[16,768]{1,0:T(8,128)(2,1)S(1)}, bf16[16,768]{1,0:T(8,128)(2,1)S(1)}, u32[]{:S(2)}, u32[]{:S(2)}) collective-permute-start(bf16[16,768]{1,0:T(8,128)(2,1)S(1)} %get-tuple-element.24), channel_id=1, source_target_pairs={{0,6},{2,4},{4,2},{6,0},{8,14},{10,12},{12,10},{14,8},{1,7},{3,5},... | collective-permute-start | bytes 73736 | tf_op jit(solution)/shard_map/ppermute | solution.py:132
  25.9 2.9 %collective-permute-start.9 = (bf16[16,1536]{1,0:T(8,128)(2,1)S(1)}, bf16[16,1536]{1,0:T(8,128)(2,1)S(1)}, u32[]{:S(2)}, u32[]{:S(2)}) collective-permute-start(bf16[16,1536]{1,0:T(8,128)(2,1)S(1)} %shard_map.88.own_ref), channel_id=1, source_target_pairs={{1,8},{3,10},{5,12},{7,14},{8,1},{10,3},{12,5},{14,7},{17,24},{19,... | collective-permute-start | bytes 147464 | tf_op jit(solution)/shard_map/ppermute | solution.py:144
  26.8 4.2 %collective-permute-start.10 = (bf16[16,1536]{1,0:T(8,128)(2,1)S(1)}, bf16[16,1536]{1,0:T(8,128)(2,1)S(1)}, u32[]{:S(2)}, u32[]{:S(2)}) collective-permute-start(bf16[16,1536]{1,0:T(8,128)(2,1)S(1)} %shard_map.88.own_ref), channel_id=1, source_target_pairs={{0,4},{1,12},{2,6},{3,14},{4,0},{5,8},{6,2},{7,10},{9,13},{8,5},{1... | collective-permute-start | bytes 147464 | tf_op jit(solution)/shard_map/ppermute | solution.py:144
  31.7 4.9 %collective-permute-start.11 = (bf16[16,768]{1,0:T(8,128)(2,1)S(1)}, bf16[16,768]{1,0:T(8,128)(2,1)S(1)}, u32[]{:S(2)}, u32[]{:S(2)}) collective-permute-start(bf16[16,768]{1,0:T(8,128)(2,1)S(1)} %shard_map.89.part_ref), channel_id=1, source_target_pairs={{0,1},{1,0},{2,3},{3,2},{4,5},{5,4},{6,7},{7,6},{8,9},{9,8},{10,11... | collective-permute-start | bytes 73736 | tf_op jit(solution)/shard_map/ppermute | solution.py:127
  35.2 3.9 %collective-permute-start.12 = (bf16[16,768]{1,0:T(8,128)(2,1)S(1)}, bf16[16,768]{1,0:T(8,128)(2,1)S(1)}, u32[]{:S(2)}, u32[]{:S(2)}) collective-permute-start(bf16[16,768]{1,0:T(8,128)(2,1)S(1)} %shard_map.89.part_ref), channel_id=1, source_target_pairs={{0,2},{2,0},{4,6},{6,4},{8,10},{10,8},{12,14},{14,12},{1,3},{3,1},... | collective-permute-start | bytes 73736 | tf_op jit(solution)/shard_map/ppermute | solution.py:132
  35.6 3.5 %collective-permute-start.13 = (bf16[16,768]{1,0:T(8,128)(2,1)S(1)}, bf16[16,768]{1,0:T(8,128)(2,1)S(1)}, u32[]{:S(2)}, u32[]{:S(2)}) collective-permute-start(bf16[16,768]{1,0:T(8,128)(2,1)S(1)} %shard_map.89.part_ref), channel_id=1, source_target_pairs={{0,3},{1,2},{2,1},{3,0},{4,7},{5,6},{6,5},{7,4},{8,11},{9,10},{10,... | collective-permute-start | bytes 73736 | tf_op jit(solution)/shard_map/ppermute | solution.py:334
  39.1 0.8 %collective-permute-start.14 = (bf16[16,1536]{1,0:T(8,128)(2,1)S(1)}, bf16[16,1536]{1,0:T(8,128)(2,1)S(1)}, u32[]{:S(2)}, u32[]{:S(2)}) collective-permute-start(bf16[16,1536]{1,0:T(8,128)(2,1)S(1)} %shard_map.90.own_ref), channel_id=1, source_target_pairs={{1,8},{3,10},{5,12},{7,14},{8,1},{10,3},{12,5},{14,7},{17,24},{19,... | collective-permute-start | bytes 147464 | tf_op jit(solution)/shard_map/ppermute | solution.py:144
  39.8 4.2 %collective-permute-start.15 = (bf16[16,1536]{1,0:T(8,128)(2,1)S(1)}, bf16[16,1536]{1,0:T(8,128)(2,1)S(1)}, u32[]{:S(2)}, u32[]{:S(2)}) collective-permute-start(bf16[16,1536]{1,0:T(8,128)(2,1)S(1)} %shard_map.90.own_ref), channel_id=1, source_target_pairs={{0,4},{1,12},{2,6},{3,14},{4,0},{5,8},{6,2},{7,10},{9,13},{8,5},{1... | collective-permute-start | bytes 147464 | tf_op jit(solution)/shard_map/ppermute | solution.py:144
  46.7 7.3 %collective-permute-start.16 = (bf16[16,3072]{1,0:T(8,128)(2,1)S(1)}, bf16[16,3072]{1,0:T(8,128)(2,1)S(1)}, u32[]{:S(2)}, u32[]{:S(2)}) collective-permute-start(bf16[16,3072]{1,0:T(8,128)(2,1)S(1)} %get-tuple-element.29), channel_id=1, source_target_pairs={{0,1},{1,0},{2,3},{3,2},{4,5},{5,4},{6,7},{7,6},{8,9},{9,8},{10,11... | collective-permute-start | bytes 294920 | tf_op jit(solution)/shard_map/ppermute | solution.py:127
  52.0 2.0 %collective-permute-start.17 = (bf16[16,3072]{1,0:T(8,128)(2,1)S(1)}, bf16[16,3072]{1,0:T(8,128)(2,1)S(1)}, u32[]{:S(2)}, u32[]{:S(2)}) collective-permute-start(bf16[16,3072]{1,0:T(8,128)(2,1)S(1)} %get-tuple-element.31), channel_id=1, source_target_pairs={{0,1},{1,0},{2,3},{3,2},{4,5},{5,4},{6,7},{7,6},{8,9},{9,8},{10,11... | collective-permute-start | bytes 294920 | tf_op jit(solution)/shard_map/ppermute | solution.py:127
  52.8 1.2 %collective-permute-start.18 = (f32[16,128]{1,0:T(8,128)S(1)}, f32[16,128]{1,0:T(8,128)S(1)}, u32[]{:S(2)}, u32[]{:S(2)}) collective-permute-start(f32[16,128]{1,0:T(8,128)S(1)} %get-tuple-element.32.refs_4_), channel_id=1, source_target_pairs={{0,1},{1,0},{2,3},{3,2},{4,5},{5,4},{6,7},{7,6},{8,9},{9,8},{10,11... | collective-permute-start | bytes 24584 | tf_op jit(solution)/shard_map/ppermute | solution.py:127
  (16 other events, 223.1 us)
